TPU v7x, 512 devices: a whole 4x4x16 slice. The times are simulated.
512 devices in a mesh: dp: 8 (over x, core), expert: 64 (over z, y).
Axes of the slice: x: 4, y: 4, z: 16, core: 2. Of those that a mesh axis runs over, the one named last changes fastest.
Arguments:
- tokens: bfloat16 [4096, 2048], P(('dp', 'expert')), may hold values from -6 to 6
- out_grad: bfloat16 [4096, 2048], P(('dp', 'expert')), may hold values from -6 to 6
- expert_ids: int32 [4096, 8], P(('dp', 'expert')), may hold values from 0 to 63, all different within a row; in each aligned block of 8 rows (0 to 7, 8 to 15, ...) at most 2 rows name the same one
- gate_values: float32 [4096, 8], P(('dp', 'expert')), may hold values from 0.05 to 1
- w_gate: bfloat16 [64, 2048, 1024], P('expert', None, 'dp'), may hold values from -0.125 to 0.125
- w_up: bfloat16 [64, 2048, 1024], P('expert', None, 'dp'), may hold values from -0.125 to 0.125
- w_down: bfloat16 [64, 1024, 2048], P('expert', 'dp'), may hold values from -0.1875 to 0.1875
Outputs:
- grad_tokens: bfloat16 [4096, 2048], P(('dp', 'expert'))
- grad_gate: float32 [64, 2048, 1024], P('expert', None, 'dp')
- grad_up: float32 [64, 2048, 1024], P('expert', None, 'dp')
- grad_down: float32 [64, 1024, 2048], P('expert', 'dp')
Inputs may be any that keep to these rules, and one draw needn't show every extreme that they name: `expert_ids`: each token names 8 different experts. Among the 8 tokens of one device (aligned blocks of 8 rows) no expert is named more than 2 times, and in every draw some expert is named exactly 2 times in some block.
All inputs are finite; a program needn't handle non-finite values.
Results may differ from a plain program's by a relative error of at most 0.014.
Values may be sent and summed in bfloat16 or wider, within the bound.
A program may use at most 64 MiB of HBM per device.

v0:
```python
import jax
import jax.numpy as jnp
from jax import lax
from jax.sharding import PartitionSpec as P


def contract_last(left_op, right_op):
    return lax.dot_general(
        left_op, right_op, (((1,), (1,)), ((), ())), preferred_element_type=jnp.float32
    )


def contract_first(left_op, right_op):
    return lax.dot_general(
        left_op, right_op, (((0,), (0,)), ((), ())), preferred_element_type=jnp.float32
    )


def slot_table(expert_ids, gate_values, expert_count, capacity):
    tok_rows, top_count = expert_ids.shape
    flat_ids = expert_ids.reshape(-1)
    onehot = (flat_ids[:, None] == jnp.arange(expert_count, dtype=jnp.int32)[None, :]).astype(
        jnp.int32
    )
    before = jnp.cumsum(onehot, axis=0) - onehot
    slot_rank = jnp.sum(before * onehot, axis=1)
    slot_index = flat_ids * capacity + slot_rank
    slot_hits = (
        slot_index[:, None] == jnp.arange(expert_count * capacity, dtype=jnp.int32)[None, :]
    ).astype(jnp.float32)
    owner_row = jnp.arange(tok_rows * top_count, dtype=jnp.int32) // top_count
    token_hits = (owner_row[:, None] == jnp.arange(tok_rows, dtype=jnp.int32)[None, :]).astype(
        jnp.float32
    )
    weighted = slot_hits * gate_values.reshape(-1)[:, None]
    return jnp.dot(weighted.T, token_hits, precision=lax.Precision.HIGHEST)


def expert_backward(x_rows, g_rows, w_pair, w_back):
    hidden_units = w_back.shape[0]
    pair_out = jnp.dot(x_rows, w_pair, preferred_element_type=jnp.float32)
    gate_pre = pair_out[:, :hidden_units]
    up_pre = pair_out[:, hidden_units:]
    sigmoid_val = jax.nn.sigmoid(gate_pre)
    silu_val = gate_pre * sigmoid_val
    activation = (silu_val * up_pre).astype(jnp.bfloat16)
    act_grad = contract_last(g_rows, w_back)
    up_grad = (act_grad * silu_val).astype(jnp.bfloat16)
    gate_grad = (act_grad * up_pre * sigmoid_val * (1.0 + gate_pre * (1.0 - sigmoid_val))).astype(
        jnp.bfloat16
    )
    pair_grads = jnp.concatenate([gate_grad, up_grad], axis=1)
    weight_pair_grad = contract_first(x_rows, pair_grads)
    weight_back_grad = contract_first(activation, g_rows)
    return (pair_grads, weight_pair_grad, weight_back_grad)


def shards(tokens, out_grad, expert_ids, gate_values, w_gate, w_up, w_down):
    expert_count = lax.axis_size("expert")
    batch_count = lax.axis_size("dp")
    tok_rows = tokens.shape[0]
    top_count = expert_ids.shape[1]
    model_width = tokens.shape[1]
    capacity = 2 * tok_rows * top_count // expert_count
    hidden_units = w_down.shape[1]
    gate_table = slot_table(expert_ids, gate_values, expert_count, capacity)
    w_pair = jnp.concatenate([w_gate[0], w_up[0]], axis=1)
    w_back = w_down[0]
    all_tokens, all_grads = (
        lax.all_gather(tokens, "dp", axis=0, tiled=True),
        lax.all_gather(out_grad, "dp", axis=0, tiled=True),
    )
    all_tables = lax.all_gather(gate_table[None], "dp", axis=0, tiled=True)
    tables_four = all_tables.reshape(batch_count, expert_count, capacity, tok_rows)
    picks = (tables_four > 0.0).astype(jnp.bfloat16)
    token_blocks = all_tokens.reshape(batch_count, tok_rows, model_width)
    grad_blocks = all_grads.reshape(batch_count, tok_rows, model_width).astype(jnp.float32)
    wide_rows = jnp.einsum(
        "pect,ptd->epcd", picks, token_blocks, preferred_element_type=jnp.float32
    ).astype(jnp.bfloat16)
    wide_grads = jnp.einsum(
        "pect,ptd->epcd", tables_four, grad_blocks, precision=lax.Precision.HIGHEST
    ).astype(jnp.bfloat16)
    got_rows, got_grads = (
        lax.all_to_all(wide_rows, "expert", split_axis=0, concat_axis=0, tiled=True),
        lax.all_to_all(wide_grads, "expert", split_axis=0, concat_axis=0, tiled=True),
    )
    total_rows = expert_count * batch_count * capacity
    pair_grads, weight_pair_grad, weight_back_grad = expert_backward(
        got_rows.reshape(total_rows, model_width),
        got_grads.reshape(total_rows, model_width),
        w_pair,
        w_back,
    )
    partial_value = contract_last(pair_grads, w_pair).astype(jnp.bfloat16)
    partial_value = partial_value.reshape(expert_count, batch_count, capacity, model_width)
    came_back = lax.all_to_all(partial_value, "expert", split_axis=0, concat_axis=0, tiled=True)
    block_sums = jnp.einsum("pect,epcd->ptd", picks, came_back, preferred_element_type=jnp.float32)
    token_grad = (
        lax.psum_scatter(block_sums.astype(jnp.bfloat16), "dp", scatter_dimension=0, tiled=True)
        .astype(jnp.float32)
        .reshape(tok_rows, model_width)
    )
    grad_tokens = token_grad.astype(jnp.bfloat16)
    grad_gate = weight_pair_grad[:, :hidden_units][None]
    grad_up = weight_pair_grad[:, hidden_units:][None]
    grad_down = weight_back_grad[None]
    return (grad_tokens, grad_gate, grad_up, grad_down)


def solution(mesh):
    return jax.shard_map(
        shards,
        mesh=mesh,
        in_specs=(
            P(("dp", "expert"), None),
            P(("dp", "expert"), None),
            P(("dp", "expert"), None),
            P(("dp", "expert"), None),
            P("expert", None, "dp"),
            P("expert", None, "dp"),
            P("expert", "dp", None),
        ),
        out_specs=(
            P(("dp", "expert"), None),
            P("expert", None, "dp"),
            P("expert", None, "dp"),
            P("expert", "dp", None),
        ),
        check_vma=False,
    )
```

profile of v0, /device:TPU:6, one launch (start us, length us, event | category | flops | bytes accessed | tf_op | source)
XLA Modules:
  0.0 706.4 jit_solution(423652889301656947)
XLA Ops:
  7.2 0.0 copy-start
  7.2 0.8 reshape.54
  8.0 0.8 mul.47
  8.8 0.1 fusion.18
  8.8 0.1 reduce_window_sum.11
  8.9 0.2 select_reduce_fusion
  9.1 0.3 fusion.16
  9.4 15.5 %all-gather = f32[1024,8]{0,1:T(8,128)S(1)} all-gather(f32[128,8]{0,1:T(8,128)S(1)} %fusion.16), channel_id=2, replica_groups=mesh['dp'=8,'expert'=64] {'dp'}, dimensions={0}, use_global_device_ids=true | all-gather | bytes 36864 | tf_op jit(solution)/shard_map/all_gather | solution.py:73
  24.9 13.2 %all_gather.11 = bf16[64,2048]{1,0:T(8,128)(2,1)S(1)} all-gather(bf16[8,2048]{1,0:T(8,128)(2,1)} %param.7), channel_id=1, replica_groups=mesh['dp'=8,'expert'=64] {'dp'}, dimensions={0}, use_global_device_ids=true | all-gather | bytes 294912 | tf_op jit(solution)/shard_map/all_gather | solution.py:70
  38.2 0.2 copy.20
  38.4 0.2 copy.21
  38.6 1.3 convert_bitcast_fusion
  39.9 6.3 copy.24
  46.2 0.0 copy-start.4
  46.2 16.2 %all-to-all-start.1 = ((bf16[64,8,2,2048]{3,2,1,0:T(2,128)(2,1)}), bf16[64,8,2,2048]{3,2,1,0:T(2,128)(2,1)}, u32[]{:S(2)}, u32[]{:S(2)}) async-start(bf16[64,8,2,2048]{3,2,1,0:T(2,128)(2,1)} %copy.24), calls=%async_computation.1 | async-start | bytes 8388608 | tf_op jit(solution)/shard_map/all_to_all | solution.py:85
  62.4 0.0 copy-done.4
  62.4 13.0 %all_gather.10 = bf16[64,2048]{1,0:T(8,128)(2,1)S(1)} all-gather(bf16[8,2048]{1,0:T(8,128)(2,1)S(1)} %copy-done.4), channel_id=1, replica_groups=mesh['dp'=8,'expert'=64] {'dp'}, dimensions={0}, use_global_device_ids=true | all-gather | bytes 294912 | tf_op jit(solution)/shard_map/all_gather | solution.py:71
  75.4 3.7 convert_bitcast_fusion.1
  79.1 6.3 copy.23
  85.4 167.4 %all-to-all-done.1 = bf16[64,8,2,2048]{3,2,1,0:T(2,128)(2,1)} async-done(((bf16[64,8,2,2048]{3,2,1,0:T(2,128)(2,1)}), bf16[64,8,2,2048]{3,2,1,0:T(2,128)(2,1)}, u32[]{:S(2)}, u32[]{:S(2)}) %all-to-all-start.1) | async-done | bytes 4194336 | tf_op jit(solution)/shard_map/all_to_all | solution.py:85
  252.8 6.3 all-to-all-start
  259.2 0.0 copy-start.2
  259.2 0.0 copy-start.3
  259.2 7.3 %reshape.59 = bf16[1024,2048]{1,0:T(8,128)(2,1)} reshape(bf16[64,8,2,2048]{3,2,1,0:T(2,128)(2,1)} %all-to-all-done.1) | data formatting | bytes 8388608 | tf_op jit(solution)/shard_map/reshape | solution.py:90
  266.4 0.0 copy-done.2
  266.5 0.0 copy-done.3
  266.5 3.5 fusion.8
  269.9 178.5 %all-to-all-done = bf16[64,8,2,2048]{3,2,1,0:T(2,128)(2,1)} async-done(((bf16[64,8,2,2048]{3,2,1,0:T(2,128)(2,1)}), bf16[64,8,2,2048]{3,2,1,0:T(2,128)(2,1)}, u32[]{:S(2)}, u32[]{:S(2)}) %all-to-all-start) | async-done | bytes 4194336 | tf_op jit(solution)/shard_map/all_to_all | solution.py:86
  448.4 7.3 %reshape.57 = bf16[1024,2048]{1,0:T(8,128)(2,1)} reshape(bf16[64,8,2,2048]{3,2,1,0:T(2,128)(2,1)} %all-to-all-done) | data formatting | bytes 8388608 | tf_op jit(solution)/shard_map/reshape | solution.py:91
  455.7 0.0 copy-done
  455.7 3.8 multiply_convert_fusion.2
  459.4 3.3 convolution_convert_fusion
  462.7 7.7 %reshape.60 = bf16[64,8,2,2048]{3,2,1,0:T(2,128)(2,1)} reshape(bf16[1024,2048]{1,0:T(8,128)(2,1)} %convolution_convert_fusion) | data formatting | bytes 8388608 | tf_op jit(solution)/shard_map/reshape | solution.py:96
  470.4 6.1 all-to-all-start.2
  476.5 0.3 reduce-scatter.2.cloned.1.call-start
  476.8 0.0 copy-start.1
  476.8 4.1 convolution_bitcast_fusion
  480.9 0.0 copy-done.1
  480.9 1.4 fusion.12
  482.2 183.4 %all-to-all-done.2 = bf16[64,8,2,2048]{3,2,1,0:T(2,128)(2,1)} async-done(((bf16[64,8,2,2048]{3,2,1,0:T(2,128)(2,1)}), bf16[64,8,2,2048]{3,2,1,0:T(2,128)(2,1)}, u32[]{:S(2)}, u32[]{:S(2)}) %all-to-all-start.2) | async-done | bytes 4194336 | tf_op jit(solution)/shard_map/all_to_all | solution.py:97
  665.6 7.3 %fusion.5 = bf16[8,8,2048]{2,1,0:T(8,128)(2,1)} fusion(pred[8,64,2,8]{1,3,2,0:T(8,128)(4,1)S(1)} %broadcast_compare_fusion, bf16[64,8,2,2048]{3,2,1,0:T(2,128)(2,1)} %all-to-all-done.2), kind=kOutput, calls=%fused_computation.7 | convolution fusion | flops 33685504 | bytes 4464640 | tf_op jit(solution)/shard_map/pect,epcd->ptd/dot_general | solution.py:98
  673.0 0.0 reduce-scatter.2.cloned.1.call-update
  673.0 1.5 slice_bitcast_fusion
  674.5 25.1 %reduce-scatter.2.cloned.1.call-done = bf16[1,8,2048]{2,1,0:T(8,128)(2,1)} async-done(((bf16[8,8,2048]{2,1,0:T(8,128)(2,1)}), bf16[1,8,2048]{2,1,0:T(8,128)(2,1)}) %reduce-scatter.2.cloned.1.call-update) | async-done | bytes 32784 | tf_op jit(solution)/shard_map/reduce_scatter | solution.py:100
  (2 shorter events, 0.0 us)
Async XLA Ops:
  7.2 448.5 %copy-start = (bf16[1,128,2048]{2,1,0:T(8,128)(2,1)S(1)}, bf16[1,128,2048]{2,1,0:T(8,128)(2,1)}, u32[]{:S(2)}) copy-start(bf16[1,128,2048]{2,1,0:T(8,128)(2,1)} %param.13) | copy-start | bytes 1572868
  46.2 16.2 %copy-start.4 = (bf16[8,2048]{1,0:T(8,128)(2,1)S(1)}, bf16[8,2048]{1,0:T(8,128)(2,1)}, u32[]{:S(2)}) copy-start(bf16[8,2048]{1,0:T(8,128)(2,1)} %param.8) | copy-start | bytes 98308
  46.2 206.6 %all-to-all-start.1 = ((bf16[64,8,2,2048]{3,2,1,0:T(2,128)(2,1)}), bf16[64,8,2,2048]{3,2,1,0:T(2,128)(2,1)}, u32[]{:S(2)}, u32[]{:S(2)}) async-start(bf16[64,8,2,2048]{3,2,1,0:T(2,128)(2,1)} %copy.24), calls=%async_computation.1 | async-start | bytes 8388608 | tf_op jit(solution)/shard_map/all_to_all | solution.py:85
  252.8 195.6 %all-to-all-start = ((bf16[64,8,2,2048]{3,2,1,0:T(2,128)(2,1)}), bf16[64,8,2,2048]{3,2,1,0:T(2,128)(2,1)}, u32[]{:S(2)}, u32[]{:S(2)}) async-start(bf16[64,8,2,2048]{3,2,1,0:T(2,128)(2,1)} %copy.23), calls=%async_computation | async-start | bytes 8388608 | tf_op jit(solution)/shard_map/all_to_all | solution.py:86
  259.2 7.3 %copy-start.2 = (bf16[1,2048,128]{2,1,0:T(8,128)(2,1)S(1)}, bf16[1,2048,128]{2,1,0:T(8,128)(2,1)}, u32[]{:S(2)}) copy-start(bf16[1,2048,128]{2,1,0:T(8,128)(2,1)} %param.12) | copy-start | bytes 1572868
  259.2 7.3 %copy-start.3 = (bf16[1,2048,128]{2,1,0:T(8,128)(2,1)S(1)}, bf16[1,2048,128]{2,1,0:T(8,128)(2,1)}, u32[]{:S(2)}) copy-start(bf16[1,2048,128]{2,1,0:T(8,128)(2,1)} %param.11) | copy-start | bytes 1572868
  470.4 195.3 %all-to-all-start.2 = ((bf16[64,8,2,2048]{3,2,1,0:T(2,128)(2,1)}), bf16[64,8,2,2048]{3,2,1,0:T(2,128)(2,1)}, u32[]{:S(2)}, u32[]{:S(2)}) async-start(bf16[64,8,2,2048]{3,2,1,0:T(2,128)(2,1)} %reshape.60), calls=%async_computation.2 | async-start | bytes 8388608 | tf_op jit(solution)/shard_map/all_to_all | solution.py:97
  476.5 223.1 %reduce-scatter.2.cloned.1.call-start = ((), (), s32[]{:S(2)}) async-start(), calls=%async_computation.4 | async-start | bytes 294912 | tf_op jit(solution)/shard_map/reduce_scatter | solution.py:100
  476.8 4.1 copy-start.1
Sparse Core Ops, SparseCore 0:
  673.1 26.3 reduce-scatter.1
where the time goes:
time: 710 us; the launch traced here: 706 us
  waiting for transfers between devices  554 us (78%)
  blocking collectives  41.8 us (6%)
  local copies, waits for them, and re-layouts  38.2 us (5%)
  starting transfers between devices  28.9 us (4%)
  matrix products  28.6 us (4%)
  between operations  14.2 us (2%)
    all_to_all x1, waiting for transfers between devices, shards(): lax.all_to_all(partial_value, 'expert', split_axis=0, concat_axis=0, tile...  183 us
    all_to_all x1, waiting for transfers between devices, shards(): lax.all_to_all(wide_grads, 'expert', split_axis=0, concat_axis=0, tiled=T...  178 us
    all_to_all x1, waiting for transfers between devices, shards(): lax.all_to_all(wide_rows, 'expert', split_axis=0, concat_axis=0, tiled=True)  167 us
    reduce_scatter x1, waiting for transfers between devices, shards(): lax.psum_scatter(block_sums.astype(jnp.bfloat16), 'dp', scatter_dimension...  25.1 us
    all_to_all x1, starting transfers between devices, shards(): lax.all_to_all(wide_rows, 'expert', split_axis=0, concat_axis=0, tiled=True)  16.2 us
    all_gather x1, blocking collectives, shards(): all_tables = lax.all_gather(gate_table[None], 'dp', axis=0, tiled=True)  15.5 us
  transfers between devices with their start and end apart: 4, of which 4 were waited for; matrix products, arithmetic and copies ran while one was open for 4% of the time, Pallas kernels for 0%

commit v1 on v0

v1 whole, which is shorter than its diff:
```python
import jax
import jax.numpy as jnp
from jax import lax
from jax.sharding import PartitionSpec as P

NZ, NY, CAP = 16, 4, 2
BF, F32 = jnp.bfloat16, jnp.float32


def contract_last(a, b):
    return lax.dot_general(a, b, (((1,), (1,)), ((), ())), preferred_element_type=F32)


def contract_first(a, b):
    return lax.dot_general(a, b, (((0,), (0,)), ((), ())), preferred_element_type=F32)


def slot_table(ids, gates):
    rows = ids.shape[0]
    col = jnp.arange(128, dtype=jnp.int32)
    hit = ids[:, :, None] == (col // CAP)[None, None, :]
    gate = jnp.sum(jnp.where(hit, gates[:, :, None], 0.0), axis=1)
    used = (gate > 0.0).astype(jnp.int32)
    t = jnp.arange(rows)
    earlier = (t[:, None] > t[None, :]).astype(jnp.int32)
    rank = jnp.sum(earlier[:, :, None] * used[None, :, :], axis=1)
    return jnp.where(rank == (col % CAP)[None, :], gate, 0.0)


def shards(tokens, out_grad, ids, gates, w_gate, w_up, w_down):
    zg = [[NY * z + y for z in range(NZ)] for y in range(NY)]
    yg = [[NY * z + y for y in range(NY)] for z in range(NZ)]
    n, d = tokens.shape
    table = slot_table(ids, gates)
    both = jnp.concatenate([tokens, out_grad], axis=0)
    allb = lax.all_gather(both, "expert", axis_index_groups=zg)
    allt = lax.all_gather(table, "expert", axis_index_groups=zg)
    z = lax.axis_index("expert") // NY
    mine = lax.dynamic_slice_in_dim(allt, z * NY * CAP, NY * CAP, axis=2)
    mine = mine.reshape(NZ, n, NY, CAP)
    picks = (mine > 0.0).astype(BF)
    gate = jnp.sum(mine, axis=1)
    x = jnp.einsum("btys,btd->ybsd", picks, allb[:, :n], preferred_element_type=F32).astype(BF)
    g = jnp.einsum("btys,btd->ybsd", picks, allb[:, n:], preferred_element_type=F32)
    g = (g * gate.transpose(1, 0, 2)[..., None]).astype(BF)
    rows = NZ * CAP
    xg = jnp.stack([x.reshape(NY, rows, d), g.reshape(NY, rows, d)], axis=1)
    xg = lax.all_to_all(xg, "expert", 0, 0, axis_index_groups=yg, tiled=True)
    xg = lax.all_gather(xg, "dp")
    ndp = xg.shape[0]
    total = ndp * NY * rows
    x = xg[:, :, 0].reshape(total, d)
    g = xg[:, :, 1].reshape(total, d)
    wg, wu, wd = w_gate[0], w_up[0], w_down[0]
    gate_pre = jnp.dot(x, wg, preferred_element_type=F32)
    up_pre = jnp.dot(x, wu, preferred_element_type=F32)
    sig = jax.nn.sigmoid(gate_pre)
    silu = gate_pre * sig
    act = (silu * up_pre).astype(BF)
    act_grad = contract_last(g, wd)
    up_grad = (act_grad * silu).astype(BF)
    gate_grad = (act_grad * up_pre * sig * (1.0 + gate_pre * (1.0 - sig))).astype(BF)
    term = (contract_last(gate_grad, wg) + contract_last(up_grad, wu)).astype(BF)
    back = lax.psum_scatter(term.reshape(ndp, NY, rows, d), "dp", scatter_dimension=0)
    back = lax.all_to_all(back, "expert", 0, 0, axis_index_groups=yg, tiled=True)
    back = back.reshape(NY, NZ, CAP, d)
    sums = jnp.einsum("btys,ybsd->btd", picks, back, preferred_element_type=F32).astype(BF)
    grad_tokens = lax.psum_scatter(sums, "expert", scatter_dimension=0, axis_index_groups=zg)
    return (
        grad_tokens.astype(BF),
        contract_first(x, gate_grad)[None],
        contract_first(x, up_grad)[None],
        contract_first(act, g)[None],
    )


def solution(mesh):
    tok = P(("dp", "expert"), None)
    col, row = P("expert", None, "dp"), P("expert", "dp", None)
    return jax.shard_map(
        shards,
        mesh=mesh,
        in_specs=(tok, tok, tok, tok, col, col, row),
        out_specs=(tok, col, col, row),
        check_vma=False,
    )
```

time: 710 us -> 313 us (0.44)
  waiting for transfers between devices: 554 us -> 195 us
  starting transfers between devices: 28.9 us -> 0.16 us
  local copies, waits for them, and re-layouts: 38.2 us -> 14.3 us
  blocking collectives: 41.8 us -> 65.4 us
  matrix products: 28.6 us -> 21.2 us
    all_to_all x3 -> x0, waiting for transfers between devices: 529 us -> none  [the longest x1 183 us: shards(): lax.all_to_all(partial_value, 'expert', split_axis=0, concat_axis=0, tile...]
    all_gather x0 -> x2, waiting for transfers between devices: none -> 90.9 us  [the longest x1 50.7 us: shards(): xg = lax.all_gather(xg, 'dp')]
    reduce_scatter x1 -> x2, waiting for transfers between devices: 25.1 us -> 104 us  [the longest x1 60.1 us: shards(): lax.psum_scatter(sums, 'expert', scatter_dimension=0, axis_index_groups=zg)]
    all_to_all x0 -> x2, blocking collectives: none -> 29.7 us  [the longest x1 15.1 us: shards(): xg = lax.all_to_all(xg, 'expert', 0, 0, axis_index_groups=yg, tiled=True)]
    all_to_all x3 -> x0, starting transfers between devices: 28.6 us -> none  [the longest x1 16.2 us: shards(): lax.all_to_all(wide_rows, 'expert', split_axis=0, concat_axis=0, tiled=True)]
    reshape x5 -> x0, local copies, waits for them, and re-layouts: 23.2 us -> none  [the longest x1 7.65 us: shards(): partial_value.reshape(expert_count, batch_count, capacity, model_width)]
    convert_element_type x2 -> x0, local copies, waits for them, and re-layouts: 12.6 us -> none  [the longest x1 6.29 us: shards(): wide_rows = jnp.einsum('pect,ptd->epcd', picks, token_blocks, preferred_e...]
    all_gather x1, local copies, waits for them, and re-layouts: 0.19 us -> 8.27 us  [shards(): xg = lax.all_gather(xg, 'dp')]
  transfers between devices with their start and end apart: 4 -> 4, of which waited for: 4 -> 4; matrix products, arithmetic and copies ran while one was open for 4% -> 3% of each run, Pallas kernels for 0% -> 0%
where the time goes in v1:
time: 313 us
  waiting for transfers between devices  195 us (62%)
  blocking collectives  65.4 us (21%)
  matrix products  21.2 us (7%)
  local copies, waits for them, and re-layouts  14.3 us (5%)
  between operations  14 us (4%)
    reduce_scatter x1, waiting for transfers between devices, shards(): lax.psum_scatter(sums, 'expert', scatter_dimension=0, axis_index_groups=zg)  60.1 us
    all_gather x1, waiting for transfers between devices, shards(): xg = lax.all_gather(xg, 'dp')  50.7 us
    reduce_scatter x1, waiting for transfers between devices, shards(): lax.psum_scatter(term.reshape(ndp, NY, rows, d), 'dp', scatter_dimension=0)  44.2 us
    all_gather x1, waiting for transfers between devices, shards(): allb = lax.all_gather(both, 'expert', axis_index_groups=zg)  40.2 us
    all_gather x1, blocking collectives, shards(): allt = lax.all_gather(table, 'expert', axis_index_groups=zg)  35.7 us
    all_to_all x1, blocking collectives, shards(): xg = lax.all_to_all(xg, 'expert', 0, 0, axis_index_groups=yg, tiled=True)  15.1 us
    all_to_all x1, blocking collectives, shards(): lax.all_to_all(back, 'expert', 0, 0, axis_index_groups=yg, tiled=True)  14.6 us
    dot_general x3, matrix products, contract_first(): lax.dot_general(a, b, (((0,), (0,)), ((), ())), preferred_element_type=F32)  8.65 us
  transfers between devices with their start and end apart: 4, of which 4 were waited for; matrix products, arithmetic and copies ran while one was open for 3% of the time, Pallas kernels for 0%

profile of v1, /device:TPU:6, one launch (start us, length us, event | category | flops | bytes accessed | tf_op | source)
XLA Modules:
  0.0 312.9 jit_solution(1028995701316753117)
XLA Ops:
  7.2 0.0 copy-start
  7.2 0.0 all-gather.5.cloned.1.call-start
  7.2 1.5 pad_maximum_fusion.1
  8.7 0.0 all-gather.5.cloned.1.call-update
  8.7 0.0 all-gather.7.cloned.1.call-start
  8.8 0.8 select_reduce_fusion
  9.6 0.1 multiply_reduce_fusion
  9.7 35.7 %all_gather.16 = f32[16,8,128]{2,1,0:T(8,128)S(1)} all-gather(f32[1,8,128]{2,1,0:T(8,128)S(1)} %bitcast_select_fusion), channel_id=1, replica_groups={{0,4,8,12,16,20,24,28,32,36,40,44,48,52,56,60},{1,5,9,13,17,21,25,29,33..., dimensions={0}, use_global_device_ids=true | all-gather | bytes 69632 | tf_op jit(solution)/shard_map/all_gather | solution.py:37
  45.5 0.1 fusion.16
  45.6 0.1 copy.54
  45.6 0.1 copy.43
  45.7 0.1 copy.53
  45.8 0.1 copy.48
  46.0 40.2 %all-gather.5.cloned.1.call-done = bf16[256,2048]{1,0:T(8,128)(2,1)} async-done(((bf16[16,2048]{1,0:T(8,128)(2,1)}), bf16[256,2048]{1,0:T(8,128)(2,1)}) %all-gather.5.cloned.1.call-update) | async-done | bytes 1048592 | tf_op jit(solution)/shard_map/all_gather | solution.py:36
  86.2 1.5 convolution_convert_fusion
  87.6 1.5 fusion.1
  89.1 0.3 copy.44
  89.4 0.3 copy.45
  89.7 0.1 pad_maximum_fusion
  89.8 15.1 %all_to_all.10 = bf16[4,2,32,2048]{3,2,1,0:T(8,128)(2,1)} all-to-all(bf16[4,2,32,2048]{3,2,1,0:T(8,128)(2,1)S(1)} %pad_maximum_fusion), channel_id=1, replica_groups={{0,1,2,3},{4,5,6,7},{8,9,10,11},{12,13,14,15},{16,17,18,19},{20,21,22,2..., dimensions={0} | all-to-all | bytes 2097152 | tf_op jit(solution)/shard_map/all_to_all | solution.py:48
  104.9 0.0 all-gather.7.cloned.1.call-update
  105.0 0.0 reduce-scatter.3.cloned.1.call-start
  105.0 50.7 %all-gather.7.cloned.1.call-done = bf16[32,2,32,2048]{3,2,1,0:T(8,128)(2,1)} async-done(((bf16[4,2,32,2048]{3,2,1,0:T(8,128)(2,1)}), bf16[32,2,32,2048]{3,2,1,0:T(8,128)(2,1)}) %all-gather.7.cloned.1.call-update) | async-done | bytes 8388624 | tf_op jit(solution)/shard_map/all_gather | solution.py:49
  155.7 8.3 %copy.46 = bf16[32,2,32,2048]{3,2,0,1:T(8,128)(2,1)} copy(bf16[32,2,32,2048]{3,2,1,0:T(8,128)(2,1)} %all-gather.7.cloned.1.call-done) | data formatting | bytes 16777216 | tf_op jit(solution)/shard_map/all_gather | solution.py:49
  164.0 4.0 %fusion.17 = (bf16[8,4,1,32,2048]{4,3,1,0,2:T(8,128)(2,1)S(1)}, bf16[8,4,1,32,2048]{4,3,1,0,2:T(8,128)(2,1)S(1)}) fusion(bf16[8,4,2,32,2048]{4,3,1,0,2:T(8,128)(2,1)} %bitcast.82), kind=kLoop, calls=%fused_computation.44 | loop fusion | bytes 16777216 | tf_op jit(solution)/shard_map/slice | solution.py:53
  168.0 0.0 copy-start.1
  168.0 0.0 copy-start.3
  168.0 0.0 copy-start.5
  168.0 1.3 fusion.5
  169.3 0.2 copy-done.5
  169.5 1.3 fusion.8
  170.7 0.5 copy-done.3
  171.2 0.0 copy-done.6
  171.2 1.3 multiply_convert_fusion.1
  172.5 1.3 fusion.3
  173.8 3.2 %add_convert_fusion = bf16[1024,2048]{1,0:T(8,128)(2,1)} fusion(f32[1024,2048]{1,0:T(8,128)S(1)} %fusion.3, bf16[1024,128]{1,0:T(8,128)(2,1)S(1)} %get-tuple-element.8, bf16[1,2048,128]{2,1,0:T(8,128)(2,1)S(1)} %copy-done.5), kind=kOutput, calls=%fused_computation | convolution fusion | flops 541065216 | bytes 13369344 | tf_op jit(solution)/shard_map/dot_general | solution.py:11
  177.0 0.0 reduce-scatter.3.cloned.1.call-update
  177.1 0.0 reduce-scatter.5.cloned.1.call-start
  177.1 44.2 %reduce-scatter.3.cloned.1.call-done = bf16[1,4,32,2048]{3,2,1,0:T(8,128)(2,1)} async-done(((bf16[8,4,32,2048]{3,2,1,0:T(8,128)(2,1)}), bf16[1,4,32,2048]{3,2,1,0:T(8,128)(2,1)}) %reduce-scatter.3.cloned.1.call-update) | async-done | bytes 524304 | tf_op jit(solution)/shard_map/reduce_scatter | solution.py:64
  221.3 14.6 %all_to_all.11 = bf16[4,32,2048]{2,1,0:T(8,128)(2,1)S(1)} all-to-all(bf16[4,32,2048]{2,1,0:T(8,128)(2,1)} %bitcast.88), channel_id=1, replica_groups={{0,1,2,3},{4,5,6,7},{8,9,10,11},{12,13,14,15},{16,17,18,19},{20,21,22,2..., dimensions={0} | all-to-all | bytes 1048576 | tf_op jit(solution)/shard_map/all_to_all | solution.py:65
  235.9 0.4 copy.47
  236.3 1.3 fusion.2
  237.6 0.0 reduce-scatter.5.cloned.1.call-update
  237.7 4.6 %convolution_bitcast_fusion.1 = f32[1,2048,128]{2,1,0:T(8,128)} fusion(bf16[1024,2048]{1,0:T(8,128)(2,1)} %bitcast.80, bf16[1024,128]{1,0:T(8,128)(2,1)S(1)} %get-tuple-element.8), kind=kOutput, calls=%fused_computation.2 | convolution fusion | flops 536870912 | bytes 5505024 | tf_op jit(solution)/shard_map/dot_general | solution.py:15
  242.3 0.0 copy-done.2
  242.3 2.3 convolution_bitcast_fusion.2
  244.6 1.8 convolution_bitcast_fusion
  246.3 60.1 %reduce-scatter.5.cloned.1.call-done = bf16[1,8,2048]{2,1,0:T(8,128)(2,1)} async-done(((bf16[16,8,2048]{2,1,0:T(8,128)(2,1)}), bf16[1,8,2048]{2,1,0:T(8,128)(2,1)}) %reduce-scatter.5.cloned.1.call-update) | async-done | bytes 32784 | tf_op jit(solution)/shard_map/reduce_scatter | solution.py:68
  (12 shorter events, 0.0 us)
Async XLA Ops:
  7.2 160.9 %copy-start = (bf16[1,2048,128]{2,1,0:T(8,128)(2,1)S(1)}, bf16[1,2048,128]{2,1,0:T(8,128)(2,1)}, u32[]{:S(2)}) copy-start(bf16[1,2048,128]{2,1,0:T(8,128)(2,1)} %param.11) | copy-start | bytes 1572868
  7.2 79.0 %all-gather.5.cloned.1.call-start = ((), (), s32[]{:S(2)}) async-start(), calls=%async_computation.6 | async-start | bytes 1114112 | tf_op jit(solution)/shard_map/all_gather | solution.py:36
  8.7 147.0 %all-gather.7.cloned.1.call-start = ((), (), s32[]{:S(2)}) async-start(), calls=%async_computation.7 | async-start | bytes 9437184 | tf_op jit(solution)/shard_map/all_gather | solution.py:49
  105.0 116.4 %reduce-scatter.3.cloned.1.call-start = ((), (), s32[]{:S(2)}) async-start(), calls=%async_computation.4 | async-start | bytes 4718592 | tf_op jit(solution)/shard_map/reduce_scatter | solution.py:64
  168.0 2.7 copy-start.1
  168.0 3.2 %copy-start.3 = (bf16[8,4,1,32,2048]{4,3,1,0,2:T(8,128)(2,1)}, bf16[8,4,1,32,2048]{4,3,1,0,2:T(8,128)(2,1)S(1)}, u32[]{:S(2)}) copy-start(bf16[8,4,1,32,2048]{4,3,1,0,2:T(8,128)(2,1)S(1)} %get-tuple-element.6) | copy-start | bytes 12582916
  168.0 1.4 copy-start.5
  169.5 1.8 copy-start.6
  177.1 129.3 %reduce-scatter.5.cloned.1.call-start = ((), (), s32[]{:S(2)}) async-start(), calls=%async_computation.5 | async-start | bytes 557056 | tf_op jit(solution)/shard_map/reduce_scatter | solution.py:68
  237.7 4.6 %copy-start.2 = (bf16[8,4,1,32,2048]{4,3,1,0,2:T(8,128)(2,1)S(1)}, bf16[8,4,1,32,2048]{4,3,1,0,2:T(8,128)(2,1)}, u32[]{:S(2)}) copy-start(bf16[8,4,1,32,2048]{4,3,1,0,2:T(8,128)(2,1)} %copy-done.1) | copy-start | bytes 12582916
  242.3 2.3 copy-start.4
Sparse Core Ops, SparseCore 0:
  10.7 75.4 all-gather.4
  105.1 50.6 all-gather.6
  177.2 44.1 reduce-scatter.2
  237.8 68.5 reduce-scatter.4

commit v2 on v1

v2 whole, which is shorter than its diff:
```python
import jax
import jax.numpy as jnp
from jax import lax
from jax.experimental import pallas as pl
from jax.experimental.pallas import tpu as pltpu
from jax.sharding import PartitionSpec as P

BF, F32, I32 = jnp.bfloat16, jnp.float32, jnp.int32
NX, NY, NZ = 4, 4, 16
TOK, TOP, D, HID = 8, 8, 2048, 128
HALF = D // 2
R = {0: 0, 1: 1, 2: 2, 3: 3, 4: 4, 5: 8, 6: 9, 7: 10, 8: 11}
L = {0: 0, 1: 5, 2: 6, 3: 7, 4: 12, 5: 13, 6: 14, 7: 15}


def contract_last(a, b):
    return lax.dot_general(a, b, (((1,), (1,)), ((), ())), preferred_element_type=F32)


def contract_first(a, b):
    return lax.dot_general(a, b, (((0,), (0,)), ((), ())), preferred_element_type=F32)


def kernel(
    ids_ref, gates_ref, tok_ref, og_ref, wg_hbm, wu_hbm, wd_hbm,
    gtok_ref, gg_ref, gu_ref, gd_ref,
    table, tt, zbuf, picks, bsend, xg, wp, wd, pg, act, term, cbuf, pbuf, dbuf, ebuf,
    fbuf, rbuf, part, sbuf, nbuf, hbuf,
    wsem, az_s, az_r, at_s, at_r, y_s, y_r, x_s, x_r, k_s, k_r, c_s, c_r,
    d_s, d_r, e_s, e_r, f_s, f_r, n_s, n_r, h_s, h_r,
):
    dp, ex = lax.axis_index("dp"), lax.axis_index("expert")
    x, c = lax.div(dp, 2), lax.rem(dp, 2)
    z, y = lax.div(ex, NY), lax.rem(ex, NY)

    def at_z(k):
        return (dp, lax.rem(z + k + NZ, NZ) * NY + y)

    def at_y(k):
        return (dp, z * NY + lax.rem(y + k, NY))

    def at_x(k):
        return (lax.rem(x + k + NX, NX) * 2 + c, ex)

    sibling = (x * 2 + 1 - c, ex)
    started = []

    def remote(src, dst, ss, rs, device):
        copy = pltpu.make_async_remote_copy(
            src_ref=src, dst_ref=dst, send_sem=ss, recv_sem=rs,
            device_id=device, device_id_type=pl.DeviceIdType.MESH,
        )
        copy.start()
        started.append(copy)
        return copy

    barrier = pltpu.get_barrier_semaphore()
    others = [at_z(k) for k in (1, 2, 3, 4, 5, -1, -2, -3, -4, -5)]
    others += [at_y(k) for k in (1, 2, 3)] + [at_x(1), at_x(-1), sibling]
    for device in others:
        pl.semaphore_signal(barrier, inc=1, device_id=device, device_id_type=pl.DeviceIdType.MESH)

    loads = [
        pltpu.make_async_copy(wg_hbm, wp.at[:, 0:HID], wsem.at[0]),
        pltpu.make_async_copy(wu_hbm, wp.at[:, HID : 2 * HID], wsem.at[1]),
        pltpu.make_async_copy(wd_hbm, wd, wsem.at[2]),
    ]
    for load in loads:
        load.start()

    zbuf[0] = jnp.concatenate([tok_ref[...].astype(F32), og_ref[...].astype(F32)], axis=0).astype(BF)
    lane = lax.broadcasted_iota(I32, (TOK, 128), 1)
    row = lax.broadcasted_iota(I32, (TOK, 128), 0)
    ids, gates = ids_ref[...], gates_ref[...]
    gate = jnp.zeros((TOK, 128), F32)
    for k in range(TOP):
        gate += jnp.where(ids[:, k : k + 1] == lax.div(lane, 2), gates[:, k : k + 1], 0.0)
    used = jnp.where(gate > 0.0, 1, 0)
    rank = jnp.zeros((TOK, 128), I32)
    for t in range(TOK - 1):
        rank += jnp.where(row > t, used[t : t + 1, :], 0)
    tile = jnp.where(rank == lax.rem(lane, 2), gate, 0.0)
    table[0, 0:8] = tile
    table[0, 8:16] = tile

    pl.semaphore_wait(barrier, len(others))

    ring = {}

    def hop(s):
        for name, slots, step in (("R", R, 1), ("L", L, -1)):
            if s not in slots:
                continue
            src, dst = slots[s - 1], slots[s]
            ring[name, s] = (
                remote(table.at[src], table.at[dst], at_s.at[dst], at_r.at[dst], at_z(step)),
                remote(zbuf.at[src], zbuf.at[dst], az_s.at[dst], az_r.at[dst], at_z(step)),
            )

    def landed(s):
        for name in "RL":
            for copy in ring.get((name, s), ()):
                copy.wait_recv()

    def pick(g):
        tt[g] = table[8 * g : 8 * g + 8].reshape(128, 128).T
        block = lax.div(lane, 16)
        pieces = []
        for j in range(NY):
            for s in range(2):
                at = 2 * (z * NY + lax.rem(y + j, NY)) + s
                pieces.append(jnp.where(block == row, tt[g, pl.ds(at, 1), :], 0.0))
        weighted = jnp.concatenate(pieces, axis=0)
        second = lax.div(lax.rem(lax.broadcasted_iota(I32, (64, 128), 1), 16), 8) == 1
        hit = weighted > 0.0
        one_x = jnp.where(hit & ~second, 1.0, 0.0).astype(BF)
        one_g = jnp.where(hit & second, 1.0, 0.0).astype(BF)
        scale = jnp.sum(jnp.where(second, weighted, 0.0), axis=1, keepdims=True)
        picks[g, 0] = one_x
        picks[g, 1] = one_g
        blocks = zbuf[8 * g : 8 * g + 8].reshape(128, D)
        rows_x = jnp.dot(one_x, blocks, preferred_element_type=F32).astype(BF)
        rows_g = (jnp.dot(one_g, blocks, preferred_element_type=F32) * scale).astype(BF)
        sent = []
        for j in range(1, NY):
            bsend[g, j - 1, 0] = rows_x[16 * j : 16 * j + 16]
            bsend[g, j - 1, 1] = rows_g[16 * j : 16 * j + 16]
            sent.append(
                remote(
                    bsend.at[g, j - 1], xg.at[g, :, 0, 0, NY - j],
                    y_s.at[g, j - 1], y_r.at[g, j - 1], at_y(j),
                )
            )
        xg[g, 0, 0, 0, 0] = rows_x[0:16]
        xg[g, 1, 0, 0, 0] = rows_g[0:16]
        return sent

    def to_sibling(g, k):
        return remote(xg.at[g, :, k, 0], xg.at[g, :, k, 1], k_s.at[g, k], k_r.at[g, k], sibling)

    def spread(g, sent):
        for copy in sent:
            copy.wait_recv()
        own = xg.at[g, :, 0, 0]
        right = remote(own, xg.at[g, :, 3, 0], x_s.at[g, 0], x_r.at[g, 0], at_x(1))
        left = remote(own, xg.at[g, :, 1, 0], x_s.at[g, 1], x_r.at[g, 1], at_x(-1))
        return right, left, [to_sibling(g, 0)]

    def forward(g, state):
        right, left, kin = state
        right.wait_recv()
        a = remote(xg.at[g, 0, 3, 0], xg.at[g, 0, 2, 0], x_s.at[g, 2], x_r.at[g, 2], at_x(1))
        kin.append(to_sibling(g, 3))
        left.wait_recv()
        b = remote(xg.at[g, 1, 1, 0], xg.at[g, 1, 2, 0], x_s.at[g, 3], x_r.at[g, 3], at_x(-1))
        kin.append(to_sibling(g, 1))
        return a, b, kin

    def last(g, state):
        a, b, kin = state
        a.wait_recv()
        b.wait_recv()
        kin.append(to_sibling(g, 2))
        return kin

    rows = NX * 2 * NY * 16

    def compute(g, kin):
        for copy in kin:
            copy.wait_recv()
        pre = jnp.dot(xg[g, 0].reshape(rows, D), wp[...], preferred_element_type=F32)
        act_grad = contract_last(xg[g, 1].reshape(rows, D), wd[...])
        gate_pre, up_pre = pre[:, :HID], pre[:, HID:]
        sig = jax.nn.sigmoid(gate_pre)
        silu = gate_pre * sig
        act[g] = (silu * up_pre).astype(BF)
        pg[g, :, HID:] = (act_grad * silu).astype(BF)
        pg[g, :, :HID] = (act_grad * up_pre * sig * (1.0 + gate_pre * (1.0 - sig))).astype(BF)

        @pl.loop(0, D // 512)
        def _(n):
            cols = pl.ds(pl.multiple_of(n * 512, 512), 512)
            out = contract_last(pg[g], wp[cols, :]).astype(BF)
            term[g, :, :, :, :, cols] = out.reshape(NX, 2, NY, 16, 512)

        return {
            k: remote(term.at[g, k, 1], cbuf.at[g, k], c_s.at[g, k], c_r.at[g, k], sibling)
            for k in (2, 1, 3, 0)
        }

    def weight_grads(g):
        @pl.loop(0, D // 256)
        def _(m):
            cols = pl.ds(pl.multiple_of(m * 256, 256), 256)
            pair = contract_first(xg[g, 0, :, :, :, :, cols].reshape(rows, 256), pg[g])
            down = contract_first(act[g], xg[g, 1, :, :, :, :, cols].reshape(rows, 256))
            if g == 0:
                gg_ref[cols, :] = pair[:, :HID]
                gu_ref[cols, :] = pair[:, HID:]
                gd_ref[:, cols] = down
            else:
                gg_ref[cols, :] += pair[:, :HID]
                gu_ref[cols, :] += pair[:, HID:]
                gd_ref[:, cols] += down

    def summed(g, k, part_of=slice(0, NY)):
        return term[g, k, 0, part_of].astype(F32) + cbuf[g, k, part_of].astype(F32)

    lo, hi = slice(0, 2), slice(2, 4)

    def back_first(g, twins):
        twins[2].wait_recv()
        pbuf[g, 1] = summed(g, 2).astype(BF)
        d_right = remote(pbuf.at[g, 1, 0:2], dbuf.at[g, 0], d_s.at[g, 0], d_r.at[g, 0], at_x(1))
        d_left = remote(pbuf.at[g, 1, 2:4], dbuf.at[g, 1], d_s.at[g, 1], d_r.at[g, 1], at_x(-1))
        twins[1].wait_recv()
        pbuf[g, 0, hi] = summed(g, 1, hi).astype(BF)
        e0 = remote(pbuf.at[g, 0, 2:4], ebuf.at[g, 0, 2:4], e_s.at[g, 0], e_r.at[g, 0], at_x(1))
        twins[3].wait_recv()
        pbuf[g, 2, lo] = summed(g, 3, lo).astype(BF)
        e1 = remote(pbuf.at[g, 2, 0:2], ebuf.at[g, 1, 0:2], e_s.at[g, 1], e_r.at[g, 1], at_x(-1))
        return d_right, d_left, e0, e1, twins[0]

    def back_second(g, state):
        d_right, d_left, e0, e1, twin = state
        d_right.wait_recv()
        pbuf[g, 0, lo] = (summed(g, 1, lo) + dbuf[g, 0].astype(F32)).astype(BF)
        e2 = remote(pbuf.at[g, 0, 0:2], ebuf.at[g, 0, 0:2], e_s.at[g, 2], e_r.at[g, 2], at_x(1))
        d_left.wait_recv()
        pbuf[g, 2, hi] = (summed(g, 3, hi) + dbuf[g, 1].astype(F32)).astype(BF)
        e3 = remote(pbuf.at[g, 2, 2:4], ebuf.at[g, 1, 2:4], e_s.at[g, 3], e_r.at[g, 3], at_x(-1))
        return e0, e1, e2, e3, twin

    def back_y(g, state):
        for copy in state:
            copy.wait_recv()
        total = (summed(g, 0) + ebuf[g, 0].astype(F32) + ebuf[g, 1].astype(F32)).astype(BF)
        fbuf[g] = total[1:NY]
        rbuf[g, 0] = total[0]
        return [
            remote(fbuf.at[g, k - 1], rbuf.at[g, NY - k], f_s.at[g, k - 1], f_r.at[g, k - 1], at_y(k))
            for k in range(1, NY)
        ]

    def combine(g, sent):
        for copy in sent:
            copy.wait_recv()
        back = rbuf[g].reshape(64, D)
        out = contract_first(picks[g, 0], back[:, :HALF]) + contract_first(picks[g, 1], back[:, HALF:])
        return out.reshape(8, 16, HALF)

    hop(1)
    for s in range(1, 4):
        landed(s)
        hop(s + 1)
    ring["R", 4][0].wait_recv()
    ring["R", 4][1].wait_recv()
    later = [ring.pop(("L", 4))]
    ring.pop(("R", 4))
    dst = R[5]
    ring["R", 5] = (
        remote(table.at[R[4]], table.at[dst], at_s.at[dst], at_r.at[dst], at_z(1)),
        remote(zbuf.at[R[4]], zbuf.at[dst], az_s.at[dst], az_r.at[dst], at_z(1)),
    )
    for copy in later[0]:
        copy.wait_recv()
    dst = L[5]
    ring["L", 5] = (
        remote(table.at[L[4]], table.at[dst], at_s.at[dst], at_r.at[dst], at_z(-1)),
        remote(zbuf.at[L[4]], zbuf.at[dst], az_s.at[dst], az_r.at[dst], at_z(-1)),
    )
    sent0 = pick(0)
    landed(5)
    hop(6)
    near = spread(0, sent0)
    for s in (6, 7):
        landed(s)
        hop(s + 1)
    landed(8)
    sent1 = pick(1)
    far = spread(1, sent1)
    near = forward(0, near)
    near = last(0, near)
    far = forward(1, far)
    for load in loads:
        load.wait()
    twins0 = compute(0, near)
    far = last(1, far)
    back0 = back_first(0, twins0)
    twins1 = compute(1, far)
    back0 = back_second(0, back0)
    back1 = back_first(1, twins1)
    y0 = back_y(0, back0)
    weight_grads(0)
    back1 = back_second(1, back1)
    s0 = combine(0, y0)
    part[...] = s0
    sbuf[0:7] = s0[1:8].astype(BF)
    into = []
    for k in range(1, 8):
        to = -k if k <= 4 else k - 4
        into.append(remote(sbuf.at[k - 1], nbuf.at[k - 1], n_s.at[k - 1], n_r.at[k - 1], at_z(to)))
    weight_grads(1)
    y1 = back_y(1, back1)
    s1 = combine(1, y1)
    chain = [None, None]
    for step in range(4):
        for side, base, toward, home in ((0, 3, -1, -5), (1, 7, 1, 4)):
            value = s1[base - step]
            if step > 0:
                chain[side].wait_recv()
                value = value + hbuf[side, step - 1].astype(F32)
            at = 7 + 4 * side + step
            sbuf[at] = value.astype(BF)
            if step < 3:
                chain[side] = remote(
                    sbuf.at[at], hbuf.at[side, step], h_s.at[side, step], h_r.at[side, step], at_z(toward)
                )
            else:
                into.append(remote(sbuf.at[at], nbuf.at[7 + side], n_s.at[7 + side], n_r.at[7 + side], at_z(home)))
    total = part[0]
    for k, copy in enumerate(into):
        copy.wait_recv()
        total = total + nbuf[k].astype(F32)
    gtok_ref[:, :HALF] = total[0:8].astype(BF)
    gtok_ref[:, HALF:] = total[8:16].astype(BF)
    for copy in started:
        copy.wait_send()


def shards(tokens, out_grad, ids, gates, w_gate, w_up, w_down):
    vmem = pl.BlockSpec(memory_space=pltpu.VMEM)
    hbm = pl.BlockSpec(memory_space=pl.ANY)
    dma = pltpu.SemaphoreType.DMA
    pair = [dma((2, 3)), dma((2, 3))]
    four = [dma((2, 4)), dma((2, 4))]
    gtok, gg, gu, gd = pl.pallas_call(
        kernel,
        out_shape=(
            jax.ShapeDtypeStruct((TOK, D), BF),
            jax.ShapeDtypeStruct((D, HID), F32),
            jax.ShapeDtypeStruct((D, HID), F32),
            jax.ShapeDtypeStruct((HID, D), F32),
        ),
        in_specs=[vmem] * 4 + [hbm] * 3,
        out_specs=(vmem,) * 4,
        scratch_shapes=[
            pltpu.VMEM((NZ, 16, 128), F32),
            pltpu.VMEM((2, 128, 128), F32),
            pltpu.VMEM((NZ, 16, D), BF),
            pltpu.VMEM((2, 2, 64, 128), BF),
            pltpu.VMEM((2, 3, 2, 16, D), BF),
            pltpu.VMEM((2, 2, NX, 2, NY, 16, D), BF),
            pltpu.VMEM((D, 2 * HID), BF),
            pltpu.VMEM((HID, D), BF),
            pltpu.VMEM((2, 512, 2 * HID), BF),
            pltpu.VMEM((2, 512, HID), BF),
            pltpu.VMEM((2, NX, 2, NY, 16, D), BF),
            pltpu.VMEM((2, NX, NY, 16, D), BF),
            pltpu.VMEM((2, 3, NY, 16, D), BF),
            pltpu.VMEM((2, 2, 2, 16, D), BF),
            pltpu.VMEM((2, 2, NY, 16, D), BF),
            pltpu.VMEM((2, 3, 16, D), BF),
            pltpu.VMEM((2, NY, 16, D), BF),
            pltpu.VMEM((8, 16, HALF), F32),
            pltpu.VMEM((15, 16, HALF), BF),
            pltpu.VMEM((9, 16, HALF), BF),
            pltpu.VMEM((2, 3, 16, HALF), BF),
            dma((3,)),
            dma((NZ,)), dma((NZ,)), dma((NZ,)), dma((NZ,)),
            *pair, *four, *four, *four,
            dma((2, 2)), dma((2, 2)), *four, *pair,
            dma((9,)), dma((9,)), *pair,
        ],
        compiler_params=pltpu.CompilerParams(
            collective_id=0, has_side_effects=True, vmem_limit_bytes=52 * 2**20
        ),
    )(ids, gates, tokens, out_grad, w_gate[0], w_up[0], w_down[0])
    return gtok, gg[None], gu[None], gd[None]


def solution(mesh):
    tok = P(("dp", "expert"), None)
    col, row = P("expert", None, "dp"), P("expert", "dp", None)
    return jax.shard_map(
        shards,
        mesh=mesh,
        in_specs=(tok, tok, tok, tok, col, col, row),
        out_specs=(tok, col, col, row),
        check_vma=False,
    )
```

time: 313 us -> 131 us (0.42)
  waiting for transfers between devices: 195 us -> 0 us
  Pallas kernels: 0 us -> 118 us
  blocking collectives: 65.4 us -> 0 us
  matrix products: 21.2 us -> 0 us
  between operations: 14 us -> 0.66 us
    pallas_call x0 -> x1, Pallas kernels: none -> 118 us  [shards(): pl.pallas_call(kernel, out_shape=(jax.ShapeDtypeStruct((TOK, D), BF), jax...]
    reduce_scatter x2 -> x0, waiting for transfers between devices: 104 us -> none  [the longest x1 60.1 us: shards(): lax.psum_scatter(sums, 'expert', scatter_dimension=0, axis_index_groups=zg)]
    all_gather x2 -> x0, waiting for transfers between devices: 90.9 us -> none  [the longest x1 50.7 us: shards(): xg = lax.all_gather(xg, 'dp')]
    all_gather x1 -> x0, blocking collectives: 35.7 us -> none  [shards(): allt = lax.all_gather(table, 'expert', axis_index_groups=zg)]
    all_to_all x2 -> x0, blocking collectives: 29.7 us -> none  [the longest x1 15.1 us: shards(): xg = lax.all_to_all(xg, 'expert', 0, 0, axis_index_groups=yg, tiled=True)]
    dot_general x11 -> x0, matrix products: 21.2 us -> none  [the longest x3 8.65 us: contract_first(): lax.dot_general(a, b, (((0,), (0,)), ((), ())), preferred_element_type=F32)]
    unnamed x16 -> x22, local copies, waits for them, and re-layouts: 0.86 us -> 11.5 us
    all_gather x1 -> x0, local copies, waits for them, and re-layouts: 8.27 us -> none  [shards(): xg = lax.all_gather(xg, 'dp')]
  transfers between devices with their start and end apart: 4 -> 0, of which waited for: 4 -> 0; matrix products, arithmetic and copies ran while one was open for 3% -> 0% of each run, Pallas kernels for 0% -> 0%
where the time goes in v2:
time: 131 us; the launch traced here: 130 us
  Pallas kernels  118 us (90%)
  local copies, waits for them, and re-layouts  11.5 us (9%)
    pallas_call x1, Pallas kernels, shards(): pl.pallas_call(kernel, out_shape=(jax.ShapeDtypeStruct((TOK, D), BF), jax...  118 us
    unnamed x22, local copies, waits for them, and re-layouts  11.5 us

profile of v2, /device:TPU:6, one launch (start us, length us, event | category | flops | bytes accessed | tf_op | source)
XLA Modules:
  0.0 129.9 jit_solution(6958790864109928575)
XLA Ops:
  0.6 0.0 copy-start.5
  0.6 0.7 copy-done.5
  1.3 0.0 copy-start
  1.3 1.0 copy-done
  2.4 0.0 copy-start.1
  2.4 1.0 copy-done.1
  3.4 0.0 copy-start.2
  3.4 1.0 copy-done.2
  4.4 0.0 copy-start.3
  4.4 0.8 copy-done.3
  5.2 0.0 copy-start.4
  5.2 0.8 copy-done.4
  6.0 0.0 copy-start.6
  6.0 0.7 copy-done.6
  6.7 117.7 %shard_map.102 = (bf16[8,2048]{1,0:T(8,128)(2,1)S(1)}, f32[2048,128]{1,0:T(8,128)}, f32[2048,128]{1,0:T(8,128)}, f32[128,2048]{1,0:T(8,128)}) custom-call(s32[8,8]{1,0:T(8,128)S(1)} %copy-done.5, f32[8,8]{1,0:T(8,128)S(1)} %copy-done.6, bf16[8,2048]{1,0:T(8,128)(2,1)S(1)} %copy-done.3, bf16[8,2048]{1,0:T(8,128)(2,1)S(1)} %copy-done.4, ...), custom_call_target="tpu_custom_call" | custom-call | tf_op jit(solution)/shard_map/pallas_call | solution.py:337
  124.3 0.6 copy.15
  124.9 0.0 copy-start.8
  124.9 2.4 %copy.16 = f32[1,2048,128]{2,1,0:T(8,128)} copy(f32[1,2048,128]{2,1,0:T(8,128)} %bitcast.11) | data formatting | bytes 2097152
  127.3 0.0 copy-done.8
  127.3 0.0 copy-start.7
  127.3 1.0 copy.17
  128.3 0.6 copy-done.7
  128.9 1.0 copy.18
Async XLA Ops:
  0.6 0.7 copy-start.5
  1.3 1.0 copy-start
  2.4 1.0 copy-start.1
  3.4 1.0 copy-start.2
  4.4 0.8 copy-start.3
  5.2 0.8 copy-start.4
  6.0 0.7 copy-start.6
  124.9 2.4 %copy-start.8 = (f32[2048,128]{1,0:T(8,128)S(1)}, f32[2048,128]{1,0:T(8,128)}, u32[]{:S(2)}) copy-start(f32[2048,128]{1,0:T(8,128)} %get-tuple-element.10) | copy-start | bytes 3145732
  127.3 1.6 %copy-start.7 = (f32[128,2048]{1,0:T(8,128)S(1)}, f32[128,2048]{1,0:T(8,128)}, u32[]{:S(2)}) copy-start(f32[128,2048]{1,0:T(8,128)} %get-tuple-element.11) | copy-start | bytes 3145732

commit v3 on v2

v3 whole, which is shorter than its diff:
```python
import jax
import jax.numpy as jnp
from jax import lax
from jax.experimental import pallas as pl
from jax.experimental.pallas import tpu as pltpu
from jax.sharding import PartitionSpec as P

BF, F32, I32 = jnp.bfloat16, jnp.float32, jnp.int32
NX, NY, NZ = 4, 4, 16
TOK, TOP, D, HID = 8, 8, 2048, 128
HALF = D // 2
R = {0: 0, 1: 1, 2: 3, 3: 5, 4: 7, 5: 9, 6: 11, 7: 13, 8: 15}
L = {0: 0, 1: 2, 2: 4, 3: 6, 4: 8, 5: 10, 6: 12, 7: 14}


def contract_last(a, b):
    return lax.dot_general(a, b, (((1,), (1,)), ((), ())), preferred_element_type=F32)


def contract_first(a, b):
    return lax.dot_general(a, b, (((0,), (0,)), ((), ())), preferred_element_type=F32)


def kernel(
    ids_hbm, gates_hbm, both_ref, wg_hbm, wu_hbm, wd_hbm,
    gtok_ref, gg_ref, gu_ref, gd_ref,
    ids_ref, gates_ref, table, tt, zbuf, weights, bsend, ybuf, xg, wp, wd, pg, act, term, cbuf, pbuf, dbuf, ebuf,
    fbuf, rbuf, part, sbuf, nbuf, hbuf,
    wsem, az_s, az_r, at_s, at_r, y_s, y_r, x_s, x_r, k_s, k_r, c_s, c_r,
    d_s, d_r, e_s, e_r, f_s, f_r, n_s, n_r, h_s, h_r,
):
    dp, ex = lax.axis_index("dp"), lax.axis_index("expert")
    x, c = lax.div(dp, 2), lax.rem(dp, 2)
    z, y = lax.div(ex, NY), lax.rem(ex, NY)

    def at_z(k):
        return (dp, lax.rem(z + k + NZ, NZ) * NY + y)

    def at_y(k):
        return (dp, z * NY + lax.rem(y + k, NY))

    def at_x(k):
        return (lax.rem(x + k + NX, NX) * 2 + c, ex)

    sibling = (x * 2 + 1 - c, ex)
    started = []

    def remote(src, dst, ss, rs, device):
        copy = pltpu.make_async_remote_copy(
            src_ref=src, dst_ref=dst, send_sem=ss, recv_sem=rs,
            device_id=device, device_id_type=pl.DeviceIdType.MESH,
        )
        copy.start()
        started.append(copy)
        return copy

    barrier = pltpu.get_barrier_semaphore()
    others = [at_z(k) for k in (1, 2, 3, 4, 5, -1, -2, -3, -4, -5)]
    others += [at_y(k) for k in (1, 2, 3)] + [at_x(1), at_x(-1), sibling]
    for device in others:
        pl.semaphore_signal(barrier, inc=1, device_id=device, device_id_type=pl.DeviceIdType.MESH)

    loads = [
        pltpu.make_async_copy(wg_hbm, wp.at[:, 0:HID], wsem.at[0]),
        pltpu.make_async_copy(wu_hbm, wp.at[:, HID : 2 * HID], wsem.at[1]),
        pltpu.make_async_copy(wd_hbm, wd, wsem.at[2]),
    ]
    small = [
        pltpu.make_async_copy(ids_hbm, ids_ref, wsem.at[3]),
        pltpu.make_async_copy(gates_hbm, gates_ref, wsem.at[4]),
    ]
    for load in small + loads:
        load.start()

    zbuf[0] = both_ref[...]
    for load in small:
        load.wait()
    lane = lax.broadcasted_iota(I32, (TOK, 128), 1)
    row = lax.broadcasted_iota(I32, (TOK, 128), 0)
    ids, gates = ids_ref[...], gates_ref[...]
    gate = jnp.zeros((TOK, 128), F32)
    for k in range(TOP):
        gate += jnp.where(ids[:, k : k + 1] == lax.div(lane, 2), gates[:, k : k + 1], 0.0)
    used = jnp.where(gate > 0.0, 1, 0)
    rank = jnp.zeros((TOK, 128), I32)
    for t in range(TOK - 1):
        rank += jnp.where(row > t, used[t : t + 1, :], 0)
    tile = jnp.where(rank == lax.rem(lane, 2), gate, 0.0)
    table[0, 0:8] = tile
    table[0, 8:16] = tile

    pl.semaphore_wait(barrier, len(others))

    ring = {}

    def hop(s):
        for name, slots, step in (("R", R, 1), ("L", L, -1)):
            if s not in slots:
                continue
            src, dst = slots[s - 1], slots[s]
            ring[name, s] = (
                remote(table.at[src], table.at[dst], at_s.at[dst], at_r.at[dst], at_z(step)),
                remote(zbuf.at[src], zbuf.at[dst], az_s.at[dst], az_r.at[dst], at_z(step)),
            )

    def landed(s):
        for name in "RL":
            for copy in ring.get((name, s), ()):
                copy.wait_recv()

    def pick(q):
        wide = jnp.concatenate([table[4 * q : 4 * q + 4].reshape(64, 128), jnp.zeros((64, 128), F32)], axis=0)
        tt[q] = wide.T
        place = lax.broadcasted_iota(I32, (8, 64), 0)
        block = lax.div(lax.broadcasted_iota(I32, (8, 64), 1), 16)
        pieces = []
        for j in range(NY):
            at = 2 * (z * NY + lax.rem(y + j, NY))
            slot = [tt[q, pl.ds(at + s, 1), 0:64] for s in range(2)]
            pieces.append(jnp.where(block == lax.rem(place, 4), jnp.where(place < 4, slot[0], slot[1]), 0.0))
        weighted = jnp.concatenate(pieces, axis=0)
        weights[q] = weighted
        second = lax.rem(lax.div(lax.broadcasted_iota(I32, (32, 64), 1), 8), 2) == 1
        hit = weighted > 0.0
        one_x = jnp.where(hit & ~second, 1.0, 0.0).astype(BF)
        one_g = jnp.where(hit & second, 1.0, 0.0).astype(BF)
        scale = jnp.sum(jnp.where(second, weighted, 0.0), axis=1, keepdims=True)
        blocks = zbuf[4 * q : 4 * q + 4].reshape(64, D)
        rows_x = jnp.dot(one_x, blocks, preferred_element_type=F32)
        rows_g = jnp.dot(one_g, blocks, preferred_element_type=F32) * scale
        sent = []
        for j in range(NY):
            cut = slice(8 * j, 8 * j + 8)
            tile = jnp.concatenate([rows_x[cut], rows_g[cut]], axis=0).astype(BF)
            if j == 0:
                ybuf[q, 0] = tile
                continue
            bsend[q, j - 1] = tile
            sent.append(
                remote(
                    bsend.at[q, j - 1], ybuf.at[q, NY - j],
                    y_s.at[q, j - 1], y_r.at[q, j - 1], at_y(j),
                )
            )
        return sent

    def held(q, *at):
        g, h = divmod(q, 2)
        return xg.at[(g, *at[:3], h)] if len(at) > 2 else xg.at[g, :, at[0], at[1], h]

    def to_sibling(q, k):
        return remote(held(q, k, 0), held(q, k, 1), k_s.at[q, k], k_r.at[q, k], sibling)

    def spread(q, sent):
        for copy in sent:
            copy.wait_recv()
        g, h = divmod(q, 2)
        tiles = [ybuf[q, j].astype(F32) for j in range(NY)]
        xg[g, 0, 0, 0, h] = jnp.concatenate([t[0:8] for t in tiles], axis=0).astype(BF)
        xg[g, 1, 0, 0, h] = jnp.concatenate([t[8:16] for t in tiles], axis=0).astype(BF)
        right = remote(held(q, 0, 0), held(q, 3, 0), x_s.at[q, 0], x_r.at[q, 0], at_x(1))
        left = remote(held(q, 0, 0), held(q, 1, 0), x_s.at[q, 1], x_r.at[q, 1], at_x(-1))
        return right, left, [to_sibling(q, 0)]

    def forward(q, state):
        right, left, kin = state
        right.wait_recv()
        a = remote(held(q, 0, 3, 0), held(q, 0, 2, 0), x_s.at[q, 2], x_r.at[q, 2], at_x(1))
        left.wait_recv()
        b = remote(held(q, 1, 1, 0), held(q, 1, 2, 0), x_s.at[q, 3], x_r.at[q, 3], at_x(-1))
        kin.append(to_sibling(q, 3))
        kin.append(to_sibling(q, 1))
        return a, b, kin

    def last(q, state):
        a, b, kin = state
        a.wait_recv()
        b.wait_recv()
        kin.append(to_sibling(q, 2))
        return kin

    rows = NX * 2 * 64

    def compute(g):
        pre = jnp.dot(xg[g, 0].reshape(rows, D), wp[...], preferred_element_type=F32)
        act_grad = contract_last(xg[g, 1].reshape(rows, D), wd[...])
        gate_pre, up_pre = pre[:, :HID], pre[:, HID:]
        sig = jax.nn.sigmoid(gate_pre)
        silu = gate_pre * sig
        act[g] = (silu * up_pre).astype(BF)
        pg[g, :, HID:] = (act_grad * silu).astype(BF)
        pg[g, :, :HID] = (act_grad * up_pre * sig * (1.0 + gate_pre * (1.0 - sig))).astype(BF)

        @pl.loop(0, D // 512)
        def _(n):
            cols = pl.ds(pl.multiple_of(n * 512, 512), 512)
            out = contract_last(pg[g], wp[cols, :]).astype(BF)
            term[g, :, :, :, :, cols] = out.reshape(NX, 2, 2, 32, 512)

        return {
            k: remote(term.at[g, k, 1], cbuf.at[g, k], c_s.at[g, k], c_r.at[g, k], sibling)
            for k in (2, 1, 3, 0)
        }

    def weight_grads(g):
        @pl.loop(0, D // 256)
        def _(m):
            cols = pl.ds(pl.multiple_of(m * 256, 256), 256)
            pair = contract_first(xg[g, 0, :, :, :, :, cols].reshape(rows, 256), pg[g])
            down = contract_first(act[g], xg[g, 1, :, :, :, :, cols].reshape(rows, 256))
            if g == 0:
                gg_ref[cols, :] = pair[:, :HID]
                gu_ref[cols, :] = pair[:, HID:]
                gd_ref[:, cols] = down
            else:
                gg_ref[cols, :] += pair[:, :HID]
                gu_ref[cols, :] += pair[:, HID:]
                gd_ref[:, cols] += down

    def summed(g, k, part_of=slice(0, 2)):
        return term[g, k, 0, part_of].astype(F32) + cbuf[g, k, part_of].astype(F32)

    lo, hi = 0, 1

    def back_first(g, twins):
        twins[2].wait_recv()
        pbuf[g, 1] = summed(g, 2).astype(BF)
        d_right = remote(pbuf.at[g, 1, 0], dbuf.at[g, 0], d_s.at[g, 0], d_r.at[g, 0], at_x(1))
        d_left = remote(pbuf.at[g, 1, 1], dbuf.at[g, 1], d_s.at[g, 1], d_r.at[g, 1], at_x(-1))
        twins[1].wait_recv()
        pbuf[g, 0, hi] = summed(g, 1, hi).astype(BF)
        e0 = remote(pbuf.at[g, 0, 1], ebuf.at[g, 0, 1], e_s.at[g, 0], e_r.at[g, 0], at_x(1))
        twins[3].wait_recv()
        pbuf[g, 2, lo] = summed(g, 3, lo).astype(BF)
        e1 = remote(pbuf.at[g, 2, 0], ebuf.at[g, 1, 0], e_s.at[g, 1], e_r.at[g, 1], at_x(-1))
        return d_right, d_left, e0, e1, twins[0]

    def back_second(g, state):
        d_right, d_left, e0, e1, twin = state
        d_right.wait_recv()
        pbuf[g, 0, lo] = (summed(g, 1, lo) + dbuf[g, 0].astype(F32)).astype(BF)
        e2 = remote(pbuf.at[g, 0, 0], ebuf.at[g, 0, 0], e_s.at[g, 2], e_r.at[g, 2], at_x(1))
        d_left.wait_recv()
        pbuf[g, 2, hi] = (summed(g, 3, hi) + dbuf[g, 1].astype(F32)).astype(BF)
        e3 = remote(pbuf.at[g, 2, 1], ebuf.at[g, 1, 1], e_s.at[g, 3], e_r.at[g, 3], at_x(-1))
        return e0, e1, e2, e3, twin

    def back_y(g, state):
        for copy in state:
            copy.wait_recv()
        total = summed(g, 0) + ebuf[g, 0].astype(F32) + ebuf[g, 1].astype(F32)
        for k in range(NY):
            cut = slice(8 * k, 8 * k + 8)
            tile = jnp.concatenate([total[0, cut], total[1, cut]], axis=0).astype(BF)
            if k == 0:
                rbuf[g, 0] = tile
            else:
                fbuf[g, k - 1] = tile
        return [
            remote(fbuf.at[g, k - 1], rbuf.at[g, NY - k], f_s.at[g, k - 1], f_r.at[g, k - 1], at_y(k))
            for k in range(1, NY)
        ]

    def combine(g, sent):
        for copy in sent:
            copy.wait_recv()
        back = rbuf[g].reshape(64, D)
        second = lax.rem(lax.div(lax.broadcasted_iota(I32, (64, 64), 1), 8), 2) == 1
        none = jnp.zeros((8, 64), F32)
        made = []
        for h in range(2):
            weighted = weights[2 * g + h]
            pieces = []
            for j in range(NY):
                piece = weighted[8 * j : 8 * j + 8]
                pieces += [piece, none] if h == 0 else [none, piece]
            hit = jnp.concatenate(pieces, axis=0) > 0.0
            one_lo = jnp.where(hit & ~second, 1.0, 0.0).astype(BF)
            one_hi = jnp.where(hit & second, 1.0, 0.0).astype(BF)
            made.append(contract_first(one_lo, back[:, :HALF]) + contract_first(one_hi, back[:, HALF:]))
        return jnp.concatenate(made, axis=0).reshape(8, 16, HALF)

    scope = jax.named_scope
    with scope("hop2"):
        hop(1)
        landed(1)
        hop(2)
        landed(2)
        hop(3)
    with scope("pick0"):
        sent0 = pick(0)
    with scope("hop3"):
        landed(3)
        hop(4)
    with scope("spread0"):
        q0 = spread(0, sent0)
    with scope("hop4"):
        landed(4)
        hop(5)
    with scope("pick1"):
        sent1 = pick(1)
    with scope("hop5"):
        landed(5)
        hop(6)
    with scope("spread1"):
        q1 = spread(1, sent1)
    with scope("hop6"):
        landed(6)
        hop(7)
    with scope("pick2"):
        sent2 = pick(2)
    with scope("forward0"):
        q0 = forward(0, q0)
    with scope("hop7"):
        landed(7)
        hop(8)
    with scope("spread2"):
        q2 = spread(2, sent2)
    with scope("hop8"):
        landed(8)
    with scope("pick3"):
        sent3 = pick(3)
    with scope("forward1"):
        q1 = forward(1, q1)
    with scope("spread3"):
        q3 = spread(3, sent3)
    with scope("last01"):
        near = last(0, q0)
        near += last(1, q1)
    with scope("forward2"):
        q2 = forward(2, q2)
    for load in loads:
        load.wait()
    with scope("kin_near"):
        for copy in near:
            copy.wait_recv()
    with scope("compute_near"):
        twins0 = compute(0)
    with scope("forward3"):
        q3 = forward(3, q3)
    with scope("last2"):
        far = last(2, q2)
    with scope("back_first_near"):
        back0 = back_first(0, twins0)
    with scope("last3"):
        far += last(3, q3)
    with scope("kin_far"):
        for copy in far:
            copy.wait_recv()
    with scope("compute_far"):
        twins1 = compute(1)
    with scope("back_second_near"):
        back0 = back_second(0, back0)
    with scope("back_first_far"):
        back1 = back_first(1, twins1)
    with scope("back_y_near"):
        y0 = back_y(0, back0)
    with scope("grads_near"):
        weight_grads(0)
    with scope("back_second_far"):
        back1 = back_second(1, back1)
    with scope("combine_near"):
        s0 = combine(0, y0)
        part[...] = s0
        sbuf[0:7] = s0[1:8].astype(BF)
        into = []
        for k in range(1, 8):
            to = -(k + 1) // 2 if k % 2 else k // 2
            into.append(remote(sbuf.at[k - 1], nbuf.at[k - 1], n_s.at[k - 1], n_r.at[k - 1], at_z(to)))
    with scope("grads_far"):
        weight_grads(1)
    with scope("back_y_far"):
        y1 = back_y(1, back1)
    with scope("combine_far"):
        s1 = combine(1, y1)
    chain = [None, None]
    with scope("chain"):
        for step in range(4):
            for side, base, toward, home in ((0, R[8], -1, -5), (1, L[7], 1, 4)):
                value = s1[base - 8 - 2 * step]
                if step > 0:
                    chain[side].wait_recv()
                    value = value + hbuf[side, step - 1].astype(F32)
                at = 7 + 4 * side + step
                sbuf[at] = value.astype(BF)
                if step < 3:
                    chain[side] = remote(
                        sbuf.at[at], hbuf.at[side, step], h_s.at[side, step], h_r.at[side, step], at_z(toward)
                    )
                else:
                    into.append(remote(sbuf.at[at], nbuf.at[7 + side], n_s.at[7 + side], n_r.at[7 + side], at_z(home)))
    with scope("finish"):
        total = part[0]
        for k, copy in enumerate(into):
            copy.wait_recv()
            total = total + nbuf[k].astype(F32)
        gtok_ref[:, :HALF] = total[0:8].astype(BF)
        gtok_ref[:, HALF:] = total[8:16].astype(BF)
        for copy in started:
            copy.wait_send()


def write_out(a_ref, b_ref, c_ref, a_out, b_out, c_out, sem):
    pairs = ((a_ref, a_out), (b_ref, b_out), (c_ref, c_out))
    copies = [pltpu.make_async_copy(i, o, sem.at[k]) for k, (i, o) in enumerate(pairs)]
    for copy in copies:
        copy.start()
    for copy in copies:
        copy.wait()


def shards(tokens, out_grad, ids, gates, w_gate, w_up, w_down):
    vmem = pl.BlockSpec(memory_space=pltpu.VMEM)
    hbm = pl.BlockSpec(memory_space=pltpu.HBM)
    dma = pltpu.SemaphoreType.DMA
    pair = [dma((2, 3)), dma((2, 3))]
    four = [dma((2, 4)), dma((2, 4))]
    both = jnp.concatenate([tokens, out_grad], axis=0)
    made = pl.pallas_call(
        kernel,
        out_shape=(
            jax.ShapeDtypeStruct((TOK, D), BF),
            pltpu.VMEM((D, HID), F32),
            pltpu.VMEM((D, HID), F32),
            pltpu.VMEM((HID, D), F32),
        ),
        in_specs=[hbm] * 2 + [vmem] + [hbm] * 3,
        out_specs=(vmem,) * 4,
        scratch_shapes=[
            pltpu.VMEM((TOK, TOP), I32),
            pltpu.VMEM((TOK, TOP), F32),
            pltpu.VMEM((NZ, 16, 128), F32),
            pltpu.VMEM((4, 128, 128), F32),
            pltpu.VMEM((NZ, 16, D), BF),
            pltpu.VMEM((4, 32, 64), F32),
            pltpu.VMEM((4, 3, 16, D), BF),
            pltpu.VMEM((4, NY, 16, D), BF),
            pltpu.VMEM((2, 2, NX, 2, 2, 32, D), BF),
            pltpu.VMEM((D, 2 * HID), BF),
            pltpu.VMEM((HID, D), BF),
            pltpu.VMEM((2, 512, 2 * HID), BF),
            pltpu.VMEM((2, 512, HID), BF),
            pltpu.VMEM((2, NX, 2, 2, 32, D), BF),
            pltpu.VMEM((2, NX, 2, 32, D), BF),
            pltpu.VMEM((2, 3, 2, 32, D), BF),
            pltpu.VMEM((2, 2, 32, D), BF),
            pltpu.VMEM((2, 2, 2, 32, D), BF),
            pltpu.VMEM((2, 3, 16, D), BF),
            pltpu.VMEM((2, NY, 16, D), BF),
            pltpu.VMEM((8, 16, HALF), F32),
            pltpu.VMEM((15, 16, HALF), BF),
            pltpu.VMEM((9, 16, HALF), BF),
            pltpu.VMEM((2, 3, 16, HALF), BF),
            dma((5,)),
            dma((NZ,)), dma((NZ,)), dma((NZ,)), dma((NZ,)),
            dma((4, 3)), dma((4, 3)), dma((4, 4)), dma((4, 4)), dma((4, 4)), dma((4, 4)), *four,
            dma((2, 2)), dma((2, 2)), *four, *pair,
            dma((9,)), dma((9,)), *pair,
        ],
        compiler_params=pltpu.CompilerParams(
            collective_id=0, has_side_effects=True, vmem_limit_bytes=52 * 2**20
        ),
    )(ids, gates, both, w_gate[0], w_up[0], w_down[0])
    gg, gu, gd = pl.pallas_call(
        write_out,
        out_shape=tuple(jax.ShapeDtypeStruct(a.shape, a.dtype) for a in made[1:]),
        in_specs=[vmem] * 3,
        out_specs=(pl.BlockSpec(memory_space=pltpu.HBM),) * 3,
        scratch_shapes=[dma((3,))],
    )(*(pltpu.with_memory_space_constraint(a, pltpu.VMEM) for a in made[1:]))
    return made[0], gg[None], gu[None], gd[None]


def solution(mesh):
    tok = P(("dp", "expert"), None)
    col, row = P("expert", None, "dp"), P("expert", "dp", None)
    return jax.shard_map(
        shards,
        mesh=mesh,
        in_specs=(tok, tok, tok, tok, col, col, row),
        out_specs=(tok, col, col, row),
        check_vma=False,
    )
```

time: 131 us -> 111 us (0.85)
  local copies, waits for them, and re-layouts: 11.5 us -> 0.62 us
  Pallas kernels: 118 us -> 108 us
  other arithmetic: 0 us -> 1.41 us
    unnamed x22 -> x3, local copies, waits for them, and re-layouts: 11.5 us -> 0.62 us
    pallas_call x1 -> x2, Pallas kernels: 118 us -> 108 us  [the longest x1 106 us: shards(): pl.pallas_call(kernel, out_shape=(jax.ShapeDtypeStruct((TOK, D), BF), plt...]
    concatenate x0 -> x1, other arithmetic: none -> 1.41 us  [shards(): both = jnp.concatenate([tokens, out_grad], axis=0)]
where the time goes in v3:
time: 111 us; the launch traced here: 110 us
  Pallas kernels  108 us (97%)
  other arithmetic  1.41 us (1%)
    pallas_call x1, Pallas kernels, shards(): pl.pallas_call(kernel, out_shape=(jax.ShapeDtypeStruct((TOK, D), BF), plt...  106 us

profile of v3, /device:TPU:6, one launch (start us, length us, event | category | flops | bytes accessed | tf_op | source)
XLA Modules:
  0.0 110.4 jit_solution(3769985378299365514)
XLA Ops:
  0.6 1.4 %pad_maximum_fusion.both_ref = bf16[16,2048]{1,0:T(8,128)(2,1)} fusion(bf16[8,2048]{1,0:T(8,128)(2,1)} %param.8, bf16[8,2048]{1,0:T(8,128)(2,1)} %param.7), kind=kLoop, calls=%fused_computation | loop fusion | flops 131072 | bytes 131072 | tf_op jit(solution)/shard_map/concatenate | solution.py:418
  2.0 106.0 %shard_map.102 = (bf16[8,2048]{1,0:T(8,128)(2,1)}, f32[2048,128]{1,0:T(8,128)S(1)}, f32[2048,128]{1,0:T(8,128)S(1)}, f32[128,2048]{1,0:T(8,128)S(1)}) custom-call(s32[8,8]{1,0:T(8,128)} %ids_hbm.1, f32[8,8]{1,0:T(8,128)} %gates_hbm.1, bf16[16,2048]{1,0:T(8,128)(2,1)} %pad_maximum_fusion.both_ref, bf16[2048,128]{1,0:T(8,128)(2,1)} %bitcast.6, ...), custom_call_target="tpu_custom_call" | custom-call | tf_op jit(solution)/shard_map/pallas_call | solution.py:419
  108.0 0.0 copy-start
  108.1 1.7 %shard_map.103 = (f32[2048,128]{1,0:T(8,128)}, f32[2048,128]{1,0:T(8,128)}, f32[128,2048]{1,0:T(8,128)}) custom-call(f32[2048,128]{1,0:T(8,128)S(1)} %get-tuple-element.12.a_ref, f32[2048,128]{1,0:T(8,128)S(1)} %get-tuple-element.13.b_ref, f32[128,2048]{1,0:T(8,128)S(1)} %get-tuple-element.14.c_ref), custom_call_target="tpu_custom_call" | custom-call | tf_op jit(solution)/shard_map/pallas_call | solution.py:464
  109.8 0.0 copy-done
  109.8 0.6 copy.12
Async XLA Ops:
  108.0 1.7 %copy-start = (bf16[8,2048]{1,0:T(8,128)(2,1)S(1)}, bf16[8,2048]{1,0:T(8,128)(2,1)}, u32[]{:S(2)}) copy-start(bf16[8,2048]{1,0:T(8,128)(2,1)} %get-tuple-element.22) | copy-start | bytes 98308

commit v4 on v3

v4 whole, which is shorter than its diff:
```python
import jax
import jax.numpy as jnp
from jax import lax
from jax.experimental import pallas as pl
from jax.experimental.pallas import tpu as pltpu
from jax.sharding import PartitionSpec as P

BF, F32, I32 = jnp.bfloat16, jnp.float32, jnp.int32
NX, NY, NZ = 4, 4, 16
TOK, TOP, D, HID = 8, 8, 2048, 128
HALF = D // 2
R = {0: 0, 1: 1, 2: 3, 3: 5, 4: 7, 5: 9, 6: 11, 7: 13, 8: 15}
L = {0: 0, 1: 2, 2: 4, 3: 6, 4: 8, 5: 10, 6: 12, 7: 14}


def contract_last(a, b):
    return lax.dot_general(a, b, (((1,), (1,)), ((), ())), preferred_element_type=F32)


def contract_first(a, b):
    return lax.dot_general(a, b, (((0,), (0,)), ((), ())), preferred_element_type=F32)


def kernel(
    ids_hbm, gates_hbm, both_hbm, wg_hbm, wu_hbm, wd_hbm,
    gtok_ref, gg_ref, gu_ref, gd_ref,
    ids_ref, gates_ref, table, tt, zbuf, weights, bsend, ybuf, xg, wp, wd, pg, act, term, cbuf, pbuf, dbuf, ebuf,
    fbuf, rbuf, part, sbuf, nbuf, hbuf,
    wsem, az_s, az_r, at_s, at_r, y_s, y_r, x_s, x_r, k_s, k_r, c_s, c_r,
    d_s, d_r, e_s, e_r, f_s, f_r, n_s, n_r, h_s, h_r,
):
    dp, ex = lax.axis_index("dp"), lax.axis_index("expert")
    x, c = lax.div(dp, 2), lax.rem(dp, 2)
    z, y = lax.div(ex, NY), lax.rem(ex, NY)

    def at_z(k):
        return (dp, lax.rem(z + k + NZ, NZ) * NY + y)

    def at_y(k):
        return (dp, z * NY + lax.rem(y + k, NY))

    def at_x(k):
        return (lax.rem(x + k + NX, NX) * 2 + c, ex)

    sibling = (x * 2 + 1 - c, ex)
    started = []

    def remote(src, dst, ss, rs, device):
        copy = pltpu.make_async_remote_copy(
            src_ref=src, dst_ref=dst, send_sem=ss, recv_sem=rs,
            device_id=device, device_id_type=pl.DeviceIdType.MESH,
        )
        copy.start()
        started.append(copy)
        return copy

    loads = [
        pltpu.make_async_copy(wg_hbm, wp.at[:, 0:HID], wsem.at[0]),
        pltpu.make_async_copy(wu_hbm, wp.at[:, HID : 2 * HID], wsem.at[1]),
        pltpu.make_async_copy(wd_hbm, wd, wsem.at[2]),
    ]
    small = [
        pltpu.make_async_copy(ids_hbm, ids_ref, wsem.at[3]),
        pltpu.make_async_copy(gates_hbm, gates_ref, wsem.at[4]),
        pltpu.make_async_copy(both_hbm, zbuf.at[0], wsem.at[5]),
    ]
    for load in small:
        load.start()

    barrier = pltpu.get_barrier_semaphore()
    others = [at_z(k) for k in (1, 2, 3, 4, 5, 6, 7, -1, -2, -3, -4, -5, -6, -7)]
    others += [at_y(k) for k in (1, 2, 3)] + [at_x(1), at_x(-1), sibling]
    for device in others:
        pl.semaphore_signal(barrier, inc=1, device_id=device, device_id_type=pl.DeviceIdType.MESH)
    for load in loads:
        load.start()

    small[2].wait()
    pl.semaphore_wait(barrier, len(others))

    ring = {}

    def hop(s, names="tz"):
        for name, slots, step in (("R", R, 1), ("L", L, -1)):
            if s not in slots:
                continue
            src, dst = slots[s - 1], slots[s]
            copies = ring.setdefault((name, s), [])
            if s == 2:
                src, step = slots[0], 2 * step
            if "z" in names:
                copies.append(remote(zbuf.at[src], zbuf.at[dst], az_s.at[dst], az_r.at[dst], at_z(step)))
            if "t" in names:
                copies.append(remote(table.at[src], table.at[dst], at_s.at[dst], at_r.at[dst], at_z(step)))

    hop(1, "z")
    hop(2, "z")
    small[0].wait()
    small[1].wait()

    lane = lax.broadcasted_iota(I32, (TOK, 128), 1)
    row = lax.broadcasted_iota(I32, (TOK, 128), 0)
    ids, gates = ids_ref[...], gates_ref[...]
    gate = jnp.zeros((TOK, 128), F32)
    for k in range(TOP):
        gate += jnp.where(ids[:, k : k + 1] == lax.div(lane, 2), gates[:, k : k + 1], 0.0)
    used = jnp.where(gate > 0.0, 1, 0)
    rank = jnp.zeros((TOK, 128), I32)
    for t in range(TOK - 1):
        rank += jnp.where(row > t, used[t : t + 1, :], 0)
    tile = jnp.where(rank == lax.rem(lane, 2), gate, 0.0)
    table[0] = tile

    hop(1, "t")
    hop(2, "t")

    def landed(s):
        for name in "RL":
            for copy in ring.get((name, s), ()):
                copy.wait_recv()

    def pick(q):
        tiles = table[4 * q : 4 * q + 4]
        twice = jnp.concatenate([tiles, tiles], axis=1).reshape(64, 128)
        wide = jnp.concatenate([twice, jnp.zeros((64, 128), F32)], axis=0)
        tt[q] = wide.T
        place = lax.broadcasted_iota(I32, (8, 64), 0)
        block = lax.div(lax.broadcasted_iota(I32, (8, 64), 1), 16)
        pieces = []
        for j in range(NY):
            at = 2 * (z * NY + lax.rem(y + j, NY))
            slot = [tt[q, pl.ds(at + s, 1), 0:64] for s in range(2)]
            pieces.append(jnp.where(block == lax.rem(place, 4), jnp.where(place < 4, slot[0], slot[1]), 0.0))
        weighted = jnp.concatenate(pieces, axis=0)
        weights[q] = weighted
        second = lax.rem(lax.div(lax.broadcasted_iota(I32, (32, 64), 1), 8), 2) == 1
        hit = weighted > 0.0
        one_x = jnp.where(hit & ~second, 1.0, 0.0).astype(BF)
        one_g = jnp.where(hit & second, 1.0, 0.0).astype(BF)
        scale = jnp.sum(jnp.where(second, weighted, 0.0), axis=1, keepdims=True)
        blocks = zbuf[4 * q : 4 * q + 4].reshape(64, D)
        rows_x = jnp.dot(one_x, blocks, preferred_element_type=F32)
        rows_g = jnp.dot(one_g, blocks, preferred_element_type=F32) * scale
        sent = []
        for j in range(NY):
            cut = slice(8 * j, 8 * j + 8)
            tile = jnp.concatenate([rows_x[cut], rows_g[cut]], axis=0).astype(BF)
            if j == 0:
                ybuf[q, 0] = tile
                continue
            bsend[q, j - 1] = tile
            sent.append(
                remote(
                    bsend.at[q, j - 1], ybuf.at[q, NY - j],
                    y_s.at[q, j - 1], y_r.at[q, j - 1], at_y(j),
                )
            )
        return sent

    def held(q, k, kin):
        return xg.at[q, :, k, kin]

    def to_sibling(q, k):
        return remote(held(q, k, 0), held(q, k, 1), k_s.at[q, k], k_r.at[q, k], sibling)

    def spread(q, sent):
        for copy in sent:
            copy.wait_recv()
        tiles = [ybuf[q, j].astype(F32) for j in range(NY)]
        xg[q, 0, 0, 0] = jnp.concatenate([t[0:8] for t in tiles], axis=0).astype(BF)
        xg[q, 1, 0, 0] = jnp.concatenate([t[8:16] for t in tiles], axis=0).astype(BF)
        right = remote(held(q, 0, 0), held(q, 3, 0), x_s.at[q, 0], x_r.at[q, 0], at_x(1))
        left = remote(held(q, 0, 0), held(q, 1, 0), x_s.at[q, 1], x_r.at[q, 1], at_x(-1))
        return right, left, [to_sibling(q, 0)]

    def forward(q, state):
        right, left, kin = state
        right.wait_recv()
        a = remote(xg.at[q, 0, 3, 0], xg.at[q, 0, 2, 0], x_s.at[q, 2], x_r.at[q, 2], at_x(1))
        left.wait_recv()
        b = remote(xg.at[q, 1, 1, 0], xg.at[q, 1, 2, 0], x_s.at[q, 3], x_r.at[q, 3], at_x(-1))
        kin.append(to_sibling(q, 3))
        kin.append(to_sibling(q, 1))
        return a, b, kin

    def last(q, state):
        a, b, kin = state
        a.wait_recv()
        b.wait_recv()
        kin.append(to_sibling(q, 2))
        return kin

    rows = NX * 2 * 32

    def compute(q, kin):
        for copy in kin:
            copy.wait_recv()
        pre = jnp.dot(xg[q, 0].reshape(rows, D), wp[...], preferred_element_type=F32)
        act_grad = contract_last(xg[q, 1].reshape(rows, D), wd[...])
        gate_pre, up_pre = pre[:, :HID], pre[:, HID:]
        sig = jax.nn.sigmoid(gate_pre)
        silu = gate_pre * sig
        act[q] = (silu * up_pre).astype(BF)
        pg[q, :, HID:] = (act_grad * silu).astype(BF)
        pg[q, :, :HID] = (act_grad * up_pre * sig * (1.0 + gate_pre * (1.0 - sig))).astype(BF)

        @pl.loop(0, D // 512)
        def _(n):
            cols = pl.ds(pl.multiple_of(n * 512, 512), 512)
            out = contract_last(pg[q], wp[cols, :]).astype(BF)
            term[q, :, :, :, cols] = out.reshape(NX, 2, 32, 512)

        return {
            k: remote(term.at[q, k, 1], cbuf.at[q, k], c_s.at[q, k], c_r.at[q, k], sibling)
            for k in (2, 1, 3, 0)
        }

    def weight_grads(g, half):
        pair = slice(2 * g, 2 * g + 2)

        @pl.loop(4 * half, 4 * half + 4)
        def _(m):
            cols = pl.ds(pl.multiple_of(m * 256, 256), 256)
            both = pg[pair].reshape(2 * rows, 2 * HID)
            wide = contract_first(xg[pair, 0, :, :, :, cols].reshape(2 * rows, 256), both)
            hidden = act[pair].reshape(2 * rows, HID)
            down = contract_first(hidden, xg[pair, 1, :, :, :, cols].reshape(2 * rows, 256))
            if g == 0:
                gg_ref[cols, :] = wide[:, :HID]
                gu_ref[cols, :] = wide[:, HID:]
                gd_ref[:, cols] = down
            else:
                gg_ref[cols, :] += wide[:, :HID]
                gu_ref[cols, :] += wide[:, HID:]
                gd_ref[:, cols] += down

    lo, hi, every = slice(0, 16), slice(16, 32), slice(0, 32)

    def summed(q, k, cut=every):
        return term[q, k, 0, cut].astype(F32) + cbuf[q, k, cut].astype(F32)

    def back_first(q, twins):
        twins[2].wait_recv()
        pbuf[q, 1] = summed(q, 2).astype(BF)
        d_right = remote(pbuf.at[q, 1, lo], dbuf.at[q, 0], d_s.at[q, 0], d_r.at[q, 0], at_x(1))
        d_left = remote(pbuf.at[q, 1, hi], dbuf.at[q, 1], d_s.at[q, 1], d_r.at[q, 1], at_x(-1))
        twins[1].wait_recv()
        pbuf[q, 0, hi] = summed(q, 1, hi).astype(BF)
        e0 = remote(pbuf.at[q, 0, hi], ebuf.at[q, 0, hi], e_s.at[q, 0], e_r.at[q, 0], at_x(1))
        twins[3].wait_recv()
        pbuf[q, 2, lo] = summed(q, 3, lo).astype(BF)
        e1 = remote(pbuf.at[q, 2, lo], ebuf.at[q, 1, lo], e_s.at[q, 1], e_r.at[q, 1], at_x(-1))
        return d_right, d_left, e0, e1, twins[0]

    def back_second(q, state):
        d_right, d_left, e0, e1, twin = state
        d_right.wait_recv()
        pbuf[q, 0, lo] = (summed(q, 1, lo) + dbuf[q, 0].astype(F32)).astype(BF)
        e2 = remote(pbuf.at[q, 0, lo], ebuf.at[q, 0, lo], e_s.at[q, 2], e_r.at[q, 2], at_x(1))
        d_left.wait_recv()
        pbuf[q, 2, hi] = (summed(q, 3, hi) + dbuf[q, 1].astype(F32)).astype(BF)
        e3 = remote(pbuf.at[q, 2, hi], ebuf.at[q, 1, hi], e_s.at[q, 3], e_r.at[q, 3], at_x(-1))
        return e0, e1, e2, e3, twin

    def back_y(q, state):
        for copy in state:
            copy.wait_recv()
        total = summed(q, 0) + ebuf[q, 0].astype(F32) + ebuf[q, 1].astype(F32)
        sent = []
        for k in range(NY):
            piece = total[8 * k : 8 * k + 8]
            tile = jnp.concatenate([piece[:, :HALF], piece[:, HALF:]], axis=0).astype(BF)
            if k == 0:
                rbuf[q, 0] = tile
                continue
            fbuf[q, k - 1] = tile
            sent.append(
                remote(fbuf.at[q, k - 1], rbuf.at[q, NY - k], f_s.at[q, k - 1], f_r.at[q, k - 1], at_y(k))
            )
        return sent

    def combine(q, sent):
        weighted = weights[q]
        second = lax.rem(lax.div(lax.broadcasted_iota(I32, (8, 64), 1), 8), 2) == 1
        pieces = []
        for j in range(NY):
            hit = weighted[8 * j : 8 * j + 8] > 0.0
            pieces += [jnp.where(hit & ~second, 1.0, 0.0), jnp.where(hit & second, 1.0, 0.0)]
        ones = jnp.concatenate(pieces, axis=0).astype(BF)
        for copy in sent:
            copy.wait_recv()
        return contract_first(ones, rbuf[q].reshape(64, HALF)).reshape(4, 16, HALF)

    into = []

    def home(k, step):
        into.append(remote(sbuf.at[k - 1], nbuf.at[len(into)], n_s.at[len(into)], n_r.at[len(into)], at_z(step)))

    def near_home(q, sent):
        made = combine(q, sent)
        first = 1 if q == 0 else 0
        if q == 0:
            part[...] = made[0]
        at = 4 * q + first
        sbuf[at - 1 : 4 * q + 3] = made[first:].astype(BF)
        for k in range(at, 4 * q + 4):
            home(k, -((k + 1) // 2) if k % 2 else k // 2)

    def pair_start(q, sent):
        made = combine(q, sent)
        at = 4 * q + 2
        sbuf[at - 1 : at + 1] = made[2:4].astype(BF)
        copies = [
            remote(sbuf.at[at], hbuf.at[q - 2, 0], h_s.at[q - 2, 0], h_r.at[q - 2, 0], at_z(-1)),
            remote(sbuf.at[at - 1], hbuf.at[q - 2, 1], h_s.at[q - 2, 1], h_r.at[q - 2, 1], at_z(1)),
        ]
        return made, copies

    def pair_home(q, state):
        made, copies = state
        for side, at in ((0, 4 * q + 1), (1, 4 * q)):
            copies[side].wait_recv()
            sbuf[at - 1] = (made[at - 4 * q] + hbuf[q - 2, side].astype(F32)).astype(BF)
            home(at, -((at + 1) // 2) if side == 0 else at // 2)

    scope = jax.named_scope
    with scope("hop2"):
        landed(2)
        hop(3)
    landed(1)
    with scope("pick0"):
        sent0 = pick(0)
    with scope("hop3"):
        landed(3)
        hop(4)
    with scope("spread0"):
        q0 = spread(0, sent0)
    with scope("hop4"):
        landed(4)
        hop(5)
    with scope("pick1"):
        sent1 = pick(1)
    with scope("hop5"):
        landed(5)
        hop(6)
    with scope("spread1"):
        q1 = spread(1, sent1)
    with scope("hop6"):
        landed(6)
        hop(7)
    with scope("pick2"):
        sent2 = pick(2)
    with scope("hop7"):
        landed(7)
        hop(8)
    with scope("forward0"):
        q0 = forward(0, q0)
    with scope("spread2"):
        q2 = spread(2, sent2)
    with scope("hop8"):
        landed(8)
    with scope("pick3"):
        sent3 = pick(3)
    with scope("forward1"):
        q1 = forward(1, q1)
    with scope("last0"):
        q0 = last(0, q0)
    with scope("loads"):
        for load in loads:
            load.wait()
    with scope("c0"):
        c0 = compute(0, q0)
    with scope("s3"):
        q3 = spread(3, sent3)
    with scope("f2"):
        q2 = forward(2, q2)
    with scope("l1"):
        q1 = last(1, q1)
    with scope("c1"):
        c1 = compute(1, q1)
    with scope("f3"):
        q3 = forward(3, q3)
    with scope("a0"):
        b0 = back_first(0, c0)
    with scope("a1"):
        b1 = back_first(1, c1)
    with scope("l2"):
        q2 = last(2, q2)
    with scope("c2"):
        c2 = compute(2, q2)
    with scope("b0"):
        b0 = back_second(0, b0)
    with scope("l3"):
        q3 = last(3, q3)
    with scope("b1"):
        b1 = back_second(1, b1)
    with scope("a2"):
        b2 = back_first(2, c2)
    with scope("c3"):
        c3 = compute(3, q3)
    with scope("y0"):
        y0 = back_y(0, b0)
    with scope("a3"):
        b3 = back_first(3, c3)
    with scope("b2"):
        b2 = back_second(2, b2)
    with scope("y1"):
        y1 = back_y(1, b1)
    with scope("h0"):
        near_home(0, y0)
    with scope("b3"):
        b3 = back_second(3, b3)
    with scope("h1"):
        near_home(1, y1)
    with scope("w00"):
        weight_grads(0, 0)
    with scope("y2"):
        y2 = back_y(2, b2)
    with scope("w01"):
        weight_grads(0, 1)
    with scope("p2"):
        p2 = pair_start(2, y2)
    with scope("y3"):
        y3 = back_y(3, b3)
    with scope("p2b"):
        pair_home(2, p2)
    with scope("p3"):
        p3 = pair_start(3, y3)
    with scope("w10"):
        weight_grads(1, 0)
    with scope("p3b"):
        pair_home(3, p3)
    with scope("w11"):
        weight_grads(1, 1)
    with scope("finish"):
        total = part[...]
        for k, copy in enumerate(into):
            copy.wait_recv()
            total = total + nbuf[k].astype(F32)
        gtok_ref[:, :HALF] = total[0:8].astype(BF)
        gtok_ref[:, HALF:] = total[8:16].astype(BF)
        for copy in started:
            copy.wait_send()


def write_out(a_ref, b_ref, c_ref, a_out, b_out, c_out, sem):
    pairs = ((a_ref, a_out), (b_ref, b_out), (c_ref, c_out))
    copies = [pltpu.make_async_copy(i, o, sem.at[k]) for k, (i, o) in enumerate(pairs)]
    for copy in copies:
        copy.start()
    for copy in copies:
        copy.wait()


def shards(tokens, out_grad, ids, gates, w_gate, w_up, w_down):
    vmem = pl.BlockSpec(memory_space=pltpu.VMEM)
    hbm = pl.BlockSpec(memory_space=pltpu.HBM)
    dma = pltpu.SemaphoreType.DMA
    three = [dma((4, 3)), dma((4, 3))]
    four = [dma((4, 4)), dma((4, 4))]
    both = jnp.concatenate([tokens, out_grad], axis=0)
    made = pl.pallas_call(
        kernel,
        out_shape=(
            jax.ShapeDtypeStruct((TOK, D), BF),
            pltpu.VMEM((D, HID), F32),
            pltpu.VMEM((D, HID), F32),
            pltpu.VMEM((HID, D), F32),
        ),
        in_specs=[hbm] * 6,
        out_specs=(vmem,) * 4,
        scratch_shapes=[
            pltpu.VMEM((TOK, TOP), I32),
            pltpu.VMEM((TOK, TOP), F32),
            pltpu.VMEM((NZ, 8, 128), F32),
            pltpu.VMEM((4, 128, 128), F32),
            pltpu.VMEM((NZ, 16, D), BF),
            pltpu.VMEM((4, 32, 64), F32),
            pltpu.VMEM((4, 3, 16, D), BF),
            pltpu.VMEM((4, NY, 16, D), BF),
            pltpu.VMEM((4, 2, NX, 2, 32, D), BF),
            pltpu.VMEM((D, 2 * HID), BF),
            pltpu.VMEM((HID, D), BF),
            pltpu.VMEM((4, 256, 2 * HID), BF),
            pltpu.VMEM((4, 256, HID), BF),
            pltpu.VMEM((4, NX, 2, 32, D), BF),
            pltpu.VMEM((4, NX, 32, D), BF),
            pltpu.VMEM((4, 3, 32, D), BF),
            pltpu.VMEM((4, 2, 16, D), BF),
            pltpu.VMEM((4, 2, 32, D), BF),
            pltpu.VMEM((4, 3, 16, HALF), BF),
            pltpu.VMEM((4, NY, 16, HALF), BF),
            pltpu.VMEM((16, HALF), F32),
            pltpu.VMEM((15, 16, HALF), BF),
            pltpu.VMEM((11, 16, HALF), BF),
            pltpu.VMEM((2, 2, 16, HALF), BF),
            dma((6,)),
            dma((NZ,)), dma((NZ,)), dma((NZ,)), dma((NZ,)),
            *three, *four, *four, *four,
            dma((4, 2)), dma((4, 2)), *four, *three,
            dma((11,)), dma((11,)), dma((2, 2)), dma((2, 2)),
        ],
        compiler_params=pltpu.CompilerParams(
            collective_id=0, has_side_effects=True, vmem_limit_bytes=52 * 2**20
        ),
    )(ids, gates, both, w_gate[0], w_up[0], w_down[0])
    gg, gu, gd = pl.pallas_call(
        write_out,
        out_shape=tuple(jax.ShapeDtypeStruct(a.shape, a.dtype) for a in made[1:]),
        in_specs=[vmem] * 3,
        out_specs=(pl.BlockSpec(memory_space=pltpu.HBM),) * 3,
        scratch_shapes=[dma((3,))],
    )(*(pltpu.with_memory_space_constraint(a, pltpu.VMEM) for a in made[1:]))
    return made[0], gg[None], gu[None], gd[None]


def solution(mesh):
    tok = P(("dp", "expert"), None)
    col, row = P("expert", None, "dp"), P("expert", "dp", None)
    return jax.shard_map(
        shards,
        mesh=mesh,
        in_specs=(tok, tok, tok, tok, col, col, row),
        out_specs=(tok, col, col, row),
        check_vma=False,
    )
```

time: 111 us -> 108 us (0.973)
  Pallas kernels: 108 us -> 104 us
    pallas_call x1, Pallas kernels: 106 us -> 102 us  [shards(): pl.pallas_call(kernel, out_shape=(jax.ShapeDtypeStruct((TOK, D), BF), plt...]
where the time goes in v4:
time: 108 us; the launch traced here: 107 us
  Pallas kernels  104 us (96%)
  other arithmetic  1.41 us (1%)
    pallas_call x1, Pallas kernels, shards(): pl.pallas_call(kernel, out_shape=(jax.ShapeDtypeStruct((TOK, D), BF), plt...  102 us

profile of v4, /device:TPU:6, one launch (start us, length us, event | category | flops | bytes accessed | tf_op | source)
XLA Modules:
  0.0 106.8 jit_solution(17925339997210393468)
XLA Ops:
  0.6 1.4 %pad_maximum_fusion.both_hbm = bf16[16,2048]{1,0:T(8,128)(2,1)} fusion(bf16[8,2048]{1,0:T(8,128)(2,1)} %param.8, bf16[8,2048]{1,0:T(8,128)(2,1)} %param.7), kind=kLoop, calls=%fused_computation | loop fusion | flops 131072 | bytes 131072 | tf_op jit(solution)/shard_map/concatenate | solution.py:461
  2.0 102.4 %shard_map.102 = (bf16[8,2048]{1,0:T(8,128)(2,1)}, f32[2048,128]{1,0:T(8,128)S(1)}, f32[2048,128]{1,0:T(8,128)S(1)}, f32[128,2048]{1,0:T(8,128)S(1)}) custom-call(s32[8,8]{1,0:T(8,128)} %ids_hbm.1, f32[8,8]{1,0:T(8,128)} %gates_hbm.1, bf16[16,2048]{1,0:T(8,128)(2,1)} %pad_maximum_fusion.both_hbm, bf16[2048,128]{1,0:T(8,128)(2,1)} %bitcast.6, ...), custom_call_target="tpu_custom_call" | custom-call | tf_op jit(solution)/shard_map/pallas_call | solution.py:462
  104.4 0.0 copy-start
  104.4 1.7 %shard_map.103 = (f32[2048,128]{1,0:T(8,128)}, f32[2048,128]{1,0:T(8,128)}, f32[128,2048]{1,0:T(8,128)}) custom-call(f32[2048,128]{1,0:T(8,128)S(1)} %get-tuple-element.12.a_ref, f32[2048,128]{1,0:T(8,128)S(1)} %get-tuple-element.13.b_ref, f32[128,2048]{1,0:T(8,128)S(1)} %get-tuple-element.14.c_ref), custom_call_target="tpu_custom_call" | custom-call | tf_op jit(solution)/shard_map/pallas_call | solution.py:507
  106.1 0.0 copy-done
  106.1 0.6 copy.12
Async XLA Ops:
  104.4 1.7 %copy-start = (bf16[8,2048]{1,0:T(8,128)(2,1)S(1)}, bf16[8,2048]{1,0:T(8,128)(2,1)}, u32[]{:S(2)}) copy-start(bf16[8,2048]{1,0:T(8,128)(2,1)} %get-tuple-element.22) | copy-start | bytes 98308

commit v5 on v4

--- a/solution.py
+++ b/solution.py
@@ -22,7 +22,7 @@
 
 
 def kernel(
-    ids_hbm, gates_hbm, both_hbm, wg_hbm, wu_hbm, wd_hbm,
+    ids_hbm, gates_hbm, tok_ref, og_ref, wg_hbm, wu_hbm, wd_hbm,
     gtok_ref, gg_ref, gu_ref, gd_ref,
     ids_ref, gates_ref, table, tt, zbuf, weights, bsend, ybuf, xg, wp, wd, pg, act, term, cbuf, pbuf, dbuf, ebuf,
     fbuf, rbuf, part, sbuf, nbuf, hbuf,
@@ -62,7 +62,6 @@
     small = [
         pltpu.make_async_copy(ids_hbm, ids_ref, wsem.at[3]),
         pltpu.make_async_copy(gates_hbm, gates_ref, wsem.at[4]),
-        pltpu.make_async_copy(both_hbm, zbuf.at[0], wsem.at[5]),
     ]
     for load in small:
         load.start()
@@ -75,7 +74,7 @@
     for load in loads:
         load.start()
 
-    small[2].wait()
+    zbuf[0] = jnp.concatenate([tok_ref[...].astype(F32), og_ref[...].astype(F32)], axis=0).astype(BF)
     pl.semaphore_wait(barrier, len(others))
 
     ring = {}
@@ -458,7 +457,6 @@
     dma = pltpu.SemaphoreType.DMA
     three = [dma((4, 3)), dma((4, 3))]
     four = [dma((4, 4)), dma((4, 4))]
-    both = jnp.concatenate([tokens, out_grad], axis=0)
     made = pl.pallas_call(
         kernel,
         out_shape=(
@@ -467,7 +465,7 @@
             pltpu.VMEM((D, HID), F32),
             pltpu.VMEM((HID, D), F32),
         ),
-        in_specs=[hbm] * 6,
+        in_specs=[hbm] * 2 + [vmem] * 2 + [hbm] * 3,
         out_specs=(vmem,) * 4,
         scratch_shapes=[
             pltpu.VMEM((TOK, TOP), I32),
@@ -494,7 +492,7 @@
             pltpu.VMEM((15, 16, HALF), BF),
             pltpu.VMEM((11, 16, HALF), BF),
             pltpu.VMEM((2, 2, 16, HALF), BF),
-            dma((6,)),
+            dma((5,)),
             dma((NZ,)), dma((NZ,)), dma((NZ,)), dma((NZ,)),
             *three, *four, *four, *four,
             dma((4, 2)), dma((4, 2)), *four, *three,
@@ -503,7 +501,7 @@
         compiler_params=pltpu.CompilerParams(
             collective_id=0, has_side_effects=True, vmem_limit_bytes=52 * 2**20
         ),
-    )(ids, gates, both, w_gate[0], w_up[0], w_down[0])
+    )(ids, gates, tokens, out_grad, w_gate[0], w_up[0], w_down[0])
     gg, gu, gd = pl.pallas_call(
         write_out,
         out_shape=tuple(jax.ShapeDtypeStruct(a.shape, a.dtype) for a in made[1:]),

time: 108 us -> 107 us (level)
  other arithmetic: 1.41 us -> 0 us
    concatenate x1 -> x0, other arithmetic: 1.41 us -> none  [shards(): both = jnp.concatenate([tokens, out_grad], axis=0)]
    pallas_call x1, Pallas kernels: 102 us -> 104 us  [shards(): pl.pallas_call(kernel, out_shape=(jax.ShapeDtypeStruct((TOK, D), BF), plt...]
where the time goes in v5:
time: 107 us
  Pallas kernels  105 us (98%)
    pallas_call x1, Pallas kernels, shards(): pl.pallas_call(kernel, out_shape=(jax.ShapeDtypeStruct((TOK, D), BF), plt...  104 us

profile of v5, /device:TPU:6, one launch (start us, length us, event | category | flops | bytes accessed | tf_op | source)
XLA Modules:
  0.0 106.7 jit_solution(8840712628329823870)
XLA Ops:
  0.6 103.7 %shard_map.102 = (bf16[8,2048]{1,0:T(8,128)(2,1)}, f32[2048,128]{1,0:T(8,128)S(1)}, f32[2048,128]{1,0:T(8,128)S(1)}, f32[128,2048]{1,0:T(8,128)S(1)}) custom-call(s32[8,8]{1,0:T(8,128)} %ids_hbm.1, f32[8,8]{1,0:T(8,128)} %gates_hbm.1, bf16[8,2048]{1,0:T(8,128)(2,1)} %tok_ref.1, bf16[8,2048]{1,0:T(8,128)(2,1)} %og_ref.1, bf16[2048,128]{1,0:T(8,128)(2,1)} %bitcast.6, ...), custom_call_target="tpu_custom_call" | custom-call | tf_op jit(solution)/shard_map/pallas_call | solution.py:460
  104.4 0.0 copy-start
  104.4 1.7 %shard_map.103 = (f32[2048,128]{1,0:T(8,128)}, f32[2048,128]{1,0:T(8,128)}, f32[128,2048]{1,0:T(8,128)}) custom-call(f32[2048,128]{1,0:T(8,128)S(1)} %get-tuple-element.12.a_ref, f32[2048,128]{1,0:T(8,128)S(1)} %get-tuple-element.13.b_ref, f32[128,2048]{1,0:T(8,128)S(1)} %get-tuple-element.14.c_ref), custom_call_target="tpu_custom_call" | custom-call | tf_op jit(solution)/shard_map/pallas_call | solution.py:505
  106.1 0.0 copy-done
  106.1 0.6 copy.12
Async XLA Ops:
  104.4 1.7 %copy-start = (bf16[8,2048]{1,0:T(8,128)(2,1)S(1)}, bf16[8,2048]{1,0:T(8,128)(2,1)}, u32[]{:S(2)}) copy-start(bf16[8,2048]{1,0:T(8,128)(2,1)} %get-tuple-element.22) | copy-start | bytes 98308
